TPU v7x, 32 devices: a whole 2x2x4 slice. The times are simulated.
32 devices in a mesh: fsdp: 32 (over z, y, x, core).
Axes of the slice: x: 2, y: 2, z: 4, core: 2. Of those that a mesh axis runs over, the one named last changes fastest.
Arguments:
- inputs: bfloat16 [8192, 2048], P('fsdp'), may hold values from -6 to 6
- doc_ids: int32 [32, 256], P('fsdp'), may hold values from 0 to 63, never falling along the last dimension, each value on 1 to 128 neighbouring positions
- attn_gain: bfloat16 [2048], P('fsdp'), may hold values from 0.5 to 1.5
- attn_shift: bfloat16 [2048], P('fsdp'), may hold values from -1.1953125 to 1.1953125
- ffn_gain: bfloat16 [2048], P('fsdp'), may hold values from 0.5 to 1.5
- ffn_shift: bfloat16 [2048], P('fsdp'), may hold values from -1.1953125 to 1.1953125
- qkv_weight: bfloat16 [2048, 6144], P('fsdp'), may hold values from -0.125 to 0.125
- qkv_bias: bfloat16 [6144], P('fsdp'), may hold values from -1.1953125 to 1.1953125
- proj_weight: bfloat16 [2048, 2048], P('fsdp'), may hold values from -0.5 to 0.5
- proj_bias: bfloat16 [2048], P('fsdp'), may hold values from -1.1953125 to 1.1953125
- up_weight: bfloat16 [2048, 8192], P('fsdp'), may hold values from -0.125 to 0.125
- up_bias: bfloat16 [8192], P('fsdp'), may hold values from -1.1953125 to 1.1953125
- down_weight: bfloat16 [8192, 2048], P('fsdp'), may hold values from -0.09375 to 0.09375
- down_bias: bfloat16 [2048], P('fsdp'), may hold values from -1.1953125 to 1.1953125
- cotangent: bfloat16 [8192, 2048], P('fsdp'), may hold values from -6 to 6
Outputs:
- layer_out: float32 [8192, 2048], P('fsdp')
- grad_inputs: float32 [8192, 2048], P('fsdp')
- grad_attn_gain: float32 [2048], P('fsdp')
- grad_attn_shift: float32 [2048], P('fsdp')
- grad_ffn_gain: float32 [2048], P('fsdp')
- grad_ffn_shift: float32 [2048], P('fsdp')
- grad_qkv_weight: float32 [2048, 6144], P('fsdp')
- grad_qkv_bias: float32 [6144], P('fsdp')
- grad_proj_weight: float32 [2048, 2048], P('fsdp')
- grad_proj_bias: float32 [2048], P('fsdp')
- grad_up_weight: float32 [2048, 8192], P('fsdp')
- grad_up_bias: float32 [8192], P('fsdp')
- grad_down_weight: float32 [8192, 2048], P('fsdp')
- grad_down_bias: float32 [2048], P('fsdp')
All inputs are finite; a program needn't handle non-finite values.
Results may differ from a plain program's by a relative error of at most 0.0069.
Values may be sent and summed in bfloat16 or wider, within the bound.
No kernel may reach another device: no remote copies, remote signals or barrier semaphores. Data moves between devices by JAX's collectives and lax.ppermute only.
A program may use at most 704 MiB of HBM per device.

v0:
```python
import functools

import jax
import jax.numpy as jnp
import numpy as np
from jax import lax
from jax.experimental import pallas as pl
from jax.experimental.pallas import tpu as pltpu
from jax.sharding import PartitionSpec as P

HEADS = 8
HEAD = 256
ROT = 64
EPS = 1e-05
MASKED = -1e30
AXIS = "fsdp"
BF16 = jnp.bfloat16
F32 = jnp.float32

SPLIT_BITS = {32: (3, 2, 0), 128: (3, 1, 0)}


def attention_kernel(qkv_ref, turn_ref, docs_row_ref, docs_col_ref, d_mixed_ref, mixed_ref, d_qkv_ref, column_ref):
    half = ROT // 2
    cosine = turn_ref[0]
    sine = turn_ref[1]
    lanes = cosine.shape[1]
    lane = lax.broadcasted_iota(jnp.int32, cosine.shape, 1)

    def swap(v):
        return jnp.where(lane < half, pltpu.roll(v, lanes - half, 1), pltpu.roll(v, half, 1))

    def turn(v, sign):
        front = v[:, :lanes]
        front = front * cosine + sign * (swap(front) * sine)
        return jnp.concatenate([front, v[:, lanes:]], axis=1)

    rq = turn(qkv_ref[:, :HEAD], 1.0).astype(BF16)
    rk = turn(qkv_ref[:, HEAD : 2 * HEAD], 1.0).astype(BF16)
    rv = qkv_ref[:, 2 * HEAD :].astype(BF16)
    count = rq.shape[0]
    here = lax.broadcasted_iota(jnp.int32, (count, count), 0)
    there = lax.broadcasted_iota(jnp.int32, (count, count), 1)
    allowed = (docs_row_ref[0] == docs_col_ref[0]) & (there <= here)
    scale = HEAD ** (-0.5)
    rows = (((1,), (1,)), ((), ()))
    firsts = (((0,), (0,)), ((), ()))
    raw = lax.dot_general(rq, rk, rows, preferred_element_type=F32)
    scores = jnp.where(allowed, raw * scale, MASKED)
    expo = jnp.exp(scores - jnp.max(scores, axis=1, keepdims=True))
    probs = expo / jnp.sum(expo, axis=1, keepdims=True)
    weights = probs.astype(BF16)
    mixed_ref[...] = jnp.dot(weights, rv, preferred_element_type=F32).astype(BF16)
    d_mixed = d_mixed_ref[...]
    d_prob = lax.dot_general(d_mixed, rv, rows, preferred_element_type=F32)
    d_score = probs * (d_prob - jnp.sum(probs * d_prob, axis=1, keepdims=True))
    d_raw = (d_score * scale).astype(BF16)
    d_rq = jnp.dot(d_raw, rk, preferred_element_type=F32)
    d_rk = lax.dot_general(d_raw, rq, firsts, preferred_element_type=F32)
    d_rv = lax.dot_general(weights, d_mixed, firsts, preferred_element_type=F32)
    d_qkv = jnp.concatenate([turn(d_rq, -1.0), turn(d_rk, -1.0), d_rv], axis=1).astype(BF16)
    d_qkv_ref[...] = d_qkv

    @pl.when(pl.program_id(0) == 0)
    def _():
        column_ref[...] = jnp.zeros_like(column_ref)

    column_ref[...] += jnp.sum(d_qkv.astype(F32), axis=0, keepdims=True)


def attention(qkv, cosine, sine, docs, d_mixed):
    rows, count = docs.shape
    turns = jnp.stack([cosine, sine])
    lanes = turns.shape[2]
    return pl.pallas_call(
        attention_kernel,
        grid=(rows,),
        in_specs=[
            pl.BlockSpec((count, 3 * HEAD), lambda i: (i, 0)),
            pl.BlockSpec((2, count, lanes), lambda i: (0, i, 0)),
            pl.BlockSpec((1, 1, count), lambda i: (i, 0, 0)),
            pl.BlockSpec((1, count, 1), lambda i: (i, 0, 0)),
            pl.BlockSpec((count, HEAD), lambda i: (i, 0)),
        ],
        out_specs=[
            pl.BlockSpec((count, HEAD), lambda i: (i, 0)),
            pl.BlockSpec((count, 3 * HEAD), lambda i: (i, 0)),
            pl.BlockSpec((1, 3 * HEAD), lambda i: (0, 0)),
        ],
        out_shape=[
            jax.ShapeDtypeStruct((rows * count, HEAD), BF16),
            jax.ShapeDtypeStruct((rows * count, 3 * HEAD), BF16),
            jax.ShapeDtypeStruct((1, 3 * HEAD), F32),
        ],
        compiler_params=pltpu.CompilerParams(vmem_limit_bytes=32 * 1024 * 1024),
        cost_estimate=pl.CostEstimate(
            flops=16 * rows * count * count * HEAD, bytes_accessed=20 * rows * count * HEAD, transcendentals=rows * count * count
        ),
    )(qkv, turns, docs[:, None, :], docs[:, :, None], d_mixed)


def times_rows(left, right):
    return jnp.einsum("tc,nc->tn", left, right, preferred_element_type=F32)


def times_tokens(left, right):
    return jnp.einsum("tn,td->nd", left, right, preferred_element_type=F32)


class Layout:
    def __init__(self, count):
        self.count = count
        self.bits = count.bit_length() - 1
        self.h_bits = SPLIT_BITS.get(count, (2, 1, 0))
        self.t_bits = tuple(b for b in range(self.bits - 1, -1, -1) if b not in self.h_bits)
        head_bits = tuple(range(self.bits - 1, self.bits - 4, -1))
        self.swap = {b: b for b in range(self.bits)}
        for a, b in zip([a for a in head_bits if a not in self.h_bits], [b for b in self.h_bits if b not in head_bits]):
            self.swap[a], self.swap[b] = b, a
        self.groups = []
        for t in range(1 << len(self.t_bits)):
            base = sum(((t >> (len(self.t_bits) - 1 - i)) & 1) << b for i, b in enumerate(self.t_bits))
            self.groups.append(
                [base | sum(((h >> (2 - i)) & 1) << b for i, b in enumerate(self.h_bits)) for h in range(8)]
            )

    def swapped(self, device):
        return sum(((device >> b) & 1) << self.swap[b] for b in range(self.bits))

    def axis(self, bit):
        return self.bits - 1 - bit

    def flip(self, value, bit):
        return lax.ppermute(value, AXIS, [(d, d ^ (1 << bit)) for d in range(self.count)])

    def exchange_heads(self, value):
        return lax.ppermute(value, AXIS, [(d, self.swapped(d)) for d in range(self.count)])

    def mine(self, bit):
        return (lax.axis_index(AXIS) >> bit) & 1

    def gather(self, value):
        pieces = {0: value}
        for bit in self.t_bits:
            pieces.update({key | (1 << bit): self.flip(piece, bit) for key, piece in list(pieces.items())})
        return pieces

    def place(self, pieces, order, shape):
        some = pieces[0]
        whole = jnp.zeros(shape, some.dtype)
        block = tuple(1 if bit is not None else size for bit, size in zip(order, shape))
        block = block + shape[len(order) :]
        for key, piece in pieces.items():
            starts = [0 if bit is None else self.mine(bit) ^ ((key >> bit) & 1) for bit in order]
            starts = starts + [0] * (len(shape) - len(order))
            whole = lax.dynamic_update_slice(whole, piece.reshape(block), starts)
        return whole

    def reduce(self, part, order):
        order = list(order)
        for bit in reversed(self.t_bits):
            axis = order.index(bit)
            mine = self.mine(bit)
            away = lax.dynamic_index_in_dim(part, 1 - mine, axis, keepdims=False).astype(BF16)
            keep = lax.dynamic_index_in_dim(part, mine, axis, keepdims=False)
            part = keep + self.flip(away, bit).astype(F32)
            order.pop(axis)
        return part

    def gather_tokens(self, value):
        pieces = [value]
        for bit in self.h_bits[:-1]:
            pieces = pieces + [self.flip(piece, bit) for piece in pieces]
        own = jnp.concatenate(pieces, axis=0)
        return jnp.concatenate([own, self.flip(own, self.h_bits[-1])], axis=0)

    def reduce_tokens(self, part):
        for bit in reversed(self.h_bits):
            half = part.shape[0] // 2
            away = part[half:].astype(BF16)
            part = part[:half].astype(F32) + self.flip(away, bit).astype(F32)
        return part

    def to_columns(self, value):
        return lax.all_to_all(value, AXIS, split_axis=0, concat_axis=0, tiled=True, axis_index_groups=self.groups)


def local_any(
    inputs,
    doc_ids,
    attn_gain,
    attn_shift,
    ffn_gain,
    ffn_shift,
    qkv_weight,
    qkv_bias,
    proj_weight,
    proj_bias,
    up_weight,
    up_bias,
    down_weight,
    down_bias,
    cotangent,
):
    n = lax.axis_size(AXIS)
    lay = Layout(n)
    bits = lay.bits
    two = (2,) * bits
    count, width = inputs.shape
    rows = width // n
    unit = up_bias.shape[0]
    hidden = unit * (n // HEADS)
    h_axes = [lay.axis(b) for b in lay.h_bits]
    t_axes = [lay.axis(b) for b in lay.t_bits]

    small = jnp.concatenate(
        [
            attn_gain,
            attn_shift,
            ffn_gain,
            ffn_shift,
            proj_bias,
            down_bias,
            qkv_bias,
            up_bias,
            doc_ids[0].astype(BF16),
        ]
    )
    small = lax.all_to_all(
        jnp.broadcast_to(small[None], (n, small.shape[0])), AXIS, split_axis=0, concat_axis=0, tiled=True
    ).astype(F32)
    sizes = [rows] * 6 + [3 * rows, unit, count]
    vectors, at = [], 0
    for size in sizes:
        vectors.append(small[:, at : at + size])
        at += size
    a_gain, a_shift, f_gain, f_shift, b_proj, b_down = [v.reshape(1, width) for v in vectors[:6]]

    heads_at = [2 + (bits - 1 - lay.swap[b]) for b in lay.h_bits]
    up_cols = up_weight.reshape((rows,) + two + (unit,))
    up_cols = up_cols.transpose([1 + a for a in h_axes] + [0] + [1 + a for a in t_axes] + [bits + 1])
    up_cols = lay.to_columns(up_cols.reshape(HEADS, rows, hidden))
    qkv_cols = qkv_weight.reshape(rows, 3, 2, 2, 2, HEAD).transpose(heads_at + [0, 1, 5])
    qkv_cols = lay.to_columns(qkv_cols.reshape(HEADS, rows, 3 * HEAD))

    x = lay.gather_tokens(inputs)
    row_order = [b if b in lay.t_bits else None for b in range(bits - 1, -1, -1)]
    w_up = lay.place(lay.gather(up_cols), row_order, two + (rows, hidden)).reshape(width, hidden)
    g = lay.gather_tokens(cotangent)
    t_two = (2,) * len(lay.t_bits)
    w_down = lay.place(lay.gather(down_weight), lay.t_bits, t_two + (unit, width)).reshape(hidden, width)
    proj_order = [lay.swap[b] for b in range(bits - 4, -1, -1)]
    w_proj = lay.place(
        lay.gather(lay.exchange_heads(proj_weight)), proj_order, t_two + (rows, width)
    ).reshape(HEAD, width)
    w_qkv = lay.place(lay.gather(qkv_cols), row_order, two + (rows, 3 * HEAD)).reshape(width, 3 * HEAD)

    b_up = vectors[7].reshape(two + (unit,)).transpose(h_axes + t_axes + [bits]).reshape(HEADS, hidden)
    b_qkv = vectors[6].reshape((3, 2, 2, 2, HEAD)).transpose([a - 1 for a in heads_at] + [0, 4]).reshape(HEADS, 3 * HEAD)
    here = sum(lay.mine(b) << (2 - i) for i, b in enumerate(lay.h_bits))
    b_up = lax.dynamic_index_in_dim(b_up, here, 0, keepdims=True)
    b_qkv = lax.dynamic_index_in_dim(b_qkv, here, 0, keepdims=True)
    me = lax.axis_index(AXIS)
    docs = []
    for j in range(HEADS):
        other = me ^ sum(((j >> i) & 1) << b for i, b in enumerate(lay.h_bits))
        docs.append(lax.dynamic_index_in_dim(vectors[8], other, 0, keepdims=True))
    docs = jnp.concatenate(docs, axis=0).astype(jnp.int32)

    index = jnp.arange(count, dtype=jnp.int32)
    same = docs[:, :, None] == docs[:, None, :]
    position = jnp.sum((same & (index[None, None, :] < index[None, :, None])).astype(jnp.int32), axis=2).reshape(-1)
    freq = 10000.0 ** (-2.0 * jnp.arange(ROT // 2, dtype=F32) / ROT)
    angle = position.astype(F32)[:, None] * freq[None, :]
    cosine, sine = jnp.cos(angle), jnp.sin(angle)
    rest = 128 - ROT
    cosine = jnp.concatenate([cosine, cosine, jnp.ones((angle.shape[0], rest), F32)], axis=1)
    sine = jnp.concatenate([-sine, sine, jnp.zeros((angle.shape[0], rest), F32)], axis=1)

    value = x.astype(F32)
    center = value - jnp.mean(value, axis=-1, keepdims=True)
    scale = lax.rsqrt(jnp.mean(center * center, axis=-1, keepdims=True) + EPS)
    xhat = center * scale
    first = (xhat * a_gain + a_shift).astype(BF16)
    second = (xhat * f_gain + f_shift).astype(BF16)

    up = jnp.dot(second, w_up, preferred_element_type=F32) + b_up
    phi_sum = 0.5 * (1.0 + lax.erf(up * (0.5**0.5)))
    act = (up * phi_sum).astype(BF16)
    slope = phi_sum + up * jnp.exp(-0.5 * up * up) * 0.3989422804014327
    part_down = times_tokens(act, g)
    d_act = times_rows(g, w_down)
    d_up = (d_act * slope).astype(BF16)
    part_up = times_tokens(second, d_up)
    d_second = times_rows(d_up, w_up)

    d_mixed = times_rows(g, w_proj).astype(BF16)
    qkv = jnp.dot(first, w_qkv, preferred_element_type=F32) + b_qkv
    mixed, d_qkv, column_qkv = attention(qkv, cosine, sine, docs, d_mixed)
    part_proj = times_tokens(mixed, g)
    part_qkv = times_tokens(first, d_qkv)
    d_first = times_rows(d_qkv, w_qkv)

    branches = jnp.dot(act, w_down, preferred_element_type=F32) + jnp.dot(mixed, w_proj, preferred_element_type=F32)
    value_own = inputs.astype(F32)
    layer_out = lay.reduce_tokens(branches) + value_own + b_proj + b_down

    edge = lay.reduce_tokens(d_first * a_gain + d_second * f_gain)
    center_own = value_own - jnp.mean(value_own, axis=-1, keepdims=True)
    scale_own = lax.rsqrt(jnp.mean(center_own * center_own, axis=-1, keepdims=True) + EPS)
    xhat_own = center_own * scale_own
    back = edge - jnp.mean(edge, axis=-1, keepdims=True) - xhat_own * jnp.mean(edge * xhat_own, axis=-1, keepdims=True)
    grad_inputs = cotangent.astype(F32) + back * scale_own

    grad_down = lay.reduce(part_down.reshape(t_two + (unit, width)), lay.t_bits)
    grad_proj = lay.reduce(part_proj.reshape(t_two + (rows, width)), proj_order)
    grad_proj = lay.exchange_heads(grad_proj.astype(BF16)).astype(F32)
    grad_up = lay.reduce(part_up.reshape(two + (rows, hidden)), row_order).reshape(HEADS, rows, hidden)
    grad_up = lay.to_columns(grad_up.astype(BF16)).astype(F32)
    axes = h_axes + t_axes
    grad_up = grad_up.reshape((2, 2, 2, rows) + t_two + (unit,))
    back_axes = [3] + [
        (axes.index(a) if axes.index(a) < 3 else axes.index(a) + 1) for a in range(bits)
    ] + [bits + 1]
    grad_up = grad_up.transpose(back_axes).reshape(rows, -1)
    grad_qkv = lay.reduce(part_qkv.reshape(two + (rows, 3 * HEAD)), row_order).reshape(HEADS, rows, 3 * HEAD)
    grad_qkv = lay.to_columns(grad_qkv.astype(BF16)).astype(F32)
    grad_qkv = grad_qkv.reshape(2, 2, 2, rows, 3, HEAD)
    grad_qkv = grad_qkv.transpose([3, 4] + [heads_at.index(a) for a in (2, 3, 4)] + [5]).reshape(rows, -1)

    column_up = jnp.sum(d_up.astype(F32), axis=0)
    column_out = jnp.sum(cotangent.astype(F32), axis=0)
    spread_up = lax.dynamic_update_slice(jnp.zeros((HEADS, hidden), F32), column_up[None], (here, 0))
    spread_up = spread_up.reshape((2,) * bits + (unit,)).transpose(
        [(axes.index(a)) for a in range(bits)] + [bits]
    )
    spread_qkv = lax.dynamic_update_slice(jnp.zeros((HEADS, 3 * HEAD), F32), column_qkv, (here, 0))
    spread_qkv = spread_qkv.reshape(2, 2, 2, 3, HEAD).transpose([3] + [heads_at.index(a) for a in (2, 3, 4)] + [4])
    sums = [
        jnp.sum(d_first * xhat, axis=0),
        jnp.sum(d_first, axis=0),
        jnp.sum(d_second * xhat, axis=0),
        jnp.sum(d_second, axis=0),
        column_out,
        spread_qkv,
        spread_up,
    ]
    sums = jnp.concatenate([s.reshape(n, -1) for s in sums], axis=1)
    sums = jnp.sum(lax.all_to_all(sums, AXIS, split_axis=0, concat_axis=0, tiled=True), axis=0)
    got, at = [], 0
    for size in [rows] * 5 + [3 * rows, unit]:
        got.append(sums[at : at + size])
        at += size
    return (
        layer_out,
        grad_inputs,
        got[0],
        got[1],
        got[2],
        got[3],
        grad_qkv,
        got[5],
        grad_proj,
        got[4],
        grad_up,
        got[6],
        grad_down,
        got[4],
    )


ZH, ZL, Y, X, CORE = 4, 3, 2, 1, 0
ROWS = (((1,), (1,)), ((), ()))
COST = 0.45e9
FIRSTS = (((0,), (0,)), ((), ()))


def after(values, *done):
    return lax.optimization_barrier(tuple(values) + done)[: len(values)]


def flip(value, bit):
    return lax.ppermute(value, AXIS, [(d, d ^ (1 << bit)) for d in range(lax.axis_size(AXIS))])


def call(body, grid, in_specs, out_specs, out_shape, args, scalars=None, limit=40, us=1.0, aliases=None):
    extra = dict(
        out_shape=out_shape,
        compiler_params=pltpu.CompilerParams(vmem_limit_bytes=limit * 1024 * 1024),
        cost_estimate=pl.CostEstimate(flops=int(us * COST), bytes_accessed=1024, transcendentals=0),
        input_output_aliases=aliases or {},
    )
    if scalars is None:
        return pl.pallas_call(body, grid=grid, in_specs=in_specs, out_specs=out_specs, **extra)(*args)
    spec = pltpu.PrefetchScalarGridSpec(num_scalar_prefetch=1, grid=grid, in_specs=in_specs, out_specs=out_specs)
    return pl.pallas_call(body, grid_spec=spec, **extra)(scalars, *args)


def shape(dims, dtype):
    return jax.ShapeDtypeStruct(dims, dtype)


def bits_of(number, count):
    return [(number >> (count - 1 - i)) & 1 for i in range(count)]


def order_columns(value, mine):
    count, width = value.shape
    wide = width // 16

    def body(mine_ref, x_ref, o_ref):
        for j in range(16):
            xr, zr, b, c = bits_of(j, 4)
            source = (zr ^ mine_ref[0]) * 8 + b * 4 + c * 2 + (xr ^ mine_ref[1])
            o_ref[:, j * wide : (j + 1) * wide] = x_ref[:, pl.ds(pl.multiple_of(source * wide, wide), wide)]

    block = pl.BlockSpec((count, width), lambda i, s: (0, 0))
    return call(body, (1,), [block], block, shape((count, width), value.dtype), (value,), mine)


def split_columns(up_weight, qkv_weight):
    rows, ff = up_weight.shape
    unit = ff // 32
    hidden = 4 * unit

    def body(u_ref, q_ref, o_ref):
        for h in range(8):
            zl, y, c = bits_of(h, 3)
            for t in range(4):
                zh, x = bits_of(t, 2)
                e = zh * 16 + zl * 8 + y * 4 + x * 2 + c
                o_ref[h, :, t * unit : (t + 1) * unit] = u_ref[:, e * unit : (e + 1) * unit]
            head = c * 4 + zl * 2 + y
            for k in range(3):
                at = (k * HEADS + head) * HEAD
                o_ref[h, :, hidden + k * HEAD : hidden + (k + 1) * HEAD] = q_ref[:, at : at + HEAD]

    def block(*dims):
        return pl.BlockSpec(dims, lambda i: (0,) * len(dims))

    return call(
        body,
        (1,),
        [block(rows, ff), block(rows, 3 * HEADS * HEAD)],
        block(8, rows, hidden + 3 * HEAD),
        shape((8, rows, hidden + 3 * HEAD), BF16),
        (up_weight, qkv_weight),
    )


def join_up(parts):
    _, rows, hidden = parts.shape
    unit = hidden // 4

    def body(p_ref, o_ref):
        for h in range(8):
            zl, y, c = bits_of(h, 3)
            for t in range(4):
                zh, x = bits_of(t, 2)
                e = zh * 16 + zl * 8 + y * 4 + x * 2 + c
                o_ref[:, e * unit : (e + 1) * unit] = p_ref[h, :, t * unit : (t + 1) * unit].astype(F32)

    return call(
        body,
        (1,),
        [pl.BlockSpec(parts.shape, lambda i: (0, 0, 0))],
        pl.BlockSpec((rows, 8 * hidden), lambda i: (0, 0)),
        shape((rows, 8 * hidden), F32),
        (parts,),
    )


def join_qkv(parts):
    _, rows, _ = parts.shape

    def body(p_ref, o_ref):
        for h in range(8):
            zl, y, c = bits_of(h, 3)
            head = c * 4 + zl * 2 + y
            for k in range(3):
                at = (k * HEADS + head) * HEAD
                o_ref[:, at : at + HEAD] = p_ref[h, :, k * HEAD : (k + 1) * HEAD].astype(F32)

    return call(
        body,
        (1,),
        [pl.BlockSpec(parts.shape, lambda i: (0, 0, 0))],
        pl.BlockSpec((rows, 3 * HEADS * HEAD), lambda i: (0, 0)),
        shape((rows, 3 * HEADS * HEAD), F32),
        (parts,),
    )


def prepare(small, place, freq, sign, rows, unit, count):
    n, _, lanes = small.shape
    width = n * rows
    up_at, gains_at = count // lanes, (count + unit) // lanes
    out_at = gains_at + 2
    qkv_at = out_at + 1

    def body(place_ref, small_ref, f_ref, s_ref, gains_ref, out_ref, up_ref, qkv_ref, docs_ref, cos_ref, sin_ref, all_ref):
        mzh, mx, mzl, my, mc, me = [place_ref[k] for k in range(6)]
        step = pl.program_id(0)

        @pl.when(step == 0)
        def _():
            all_ref[...] = small_ref[...].astype(F32)
            gains_ref[...] = jnp.zeros_like(gains_ref)

            for j in range(16):
                xr, zr, b, c = bits_of(j, 4)
                source = 2 * ((zr ^ mzh) * 8 + b * 4 + c * 2 + (xr ^ mx))
                here = slice(2 * j * rows, 2 * (j + 1) * rows)
                left, right = all_ref[source], all_ref[source + 1]
                for k in range(4):
                    at, part = gains_at + k // 2, slice(k % 2 * rows, (k % 2 + 1) * rows)
                    gains_ref[k : k + 1, here] = jnp.concatenate([left[at : at + 1, part], right[at : at + 1, part]], axis=1)
                left, right = [v[:, :rows] + v[:, rows:] for v in (all_ref[2 * j, out_at : out_at + 1], all_ref[2 * j + 1, out_at : out_at + 1])]
                out_ref[:, here] = jnp.concatenate([left, right], axis=1)
            for t in range(4):
                zh, x = bits_of(t, 2)
                device = zh * 16 + mzl * 8 + my * 4 + x * 2 + mc
                mine_up = all_ref[device]
                for k in range(unit // lanes):
                    up_ref[:, t * unit + k * lanes : t * unit + (k + 1) * lanes] = mine_up[up_at + k : up_at + k + 1]
            head = mc * 4 + mzl * 2 + my
            for k in range(3 * HEAD // rows):
                chunk = (k // (HEAD // rows) * HEADS + head) * (HEAD // rows) + k % (HEAD // rows)
                third = all_ref[chunk // 3]
                part = lax.rem(chunk, 3)
                first, last = third[qkv_at : qkv_at + 1], third[qkv_at + 1 : qkv_at + 2]
                qkv_ref[:, k * rows : (k + 1) * rows] = jnp.where(
                    part == 0, first[:, :rows], jnp.where(part == 1, first[:, rows:], last[:, :rows])
                )

        other = me ^ (((step & 1) << ZL) | (((step >> 1) & 1) << Y) | (((step >> 2) & 1) << CORE))
        held = all_ref[other]
        docs = jnp.concatenate([held[k : k + 1] for k in range(count // lanes)], axis=1)
        docs_ref[0] = docs
        across = jnp.broadcast_to(docs, (count, count))
        here = lax.broadcasted_iota(jnp.int32, (count, count), 0)
        there = lax.broadcasted_iota(jnp.int32, (count, count), 1)
        earlier = (across == across.T) & (there < here)
        position = jnp.sum(earlier.astype(F32), axis=1, keepdims=True)
        angle = position * f_ref[...]
        cos_ref[...] = jnp.cos(angle)
        sin_ref[...] = jnp.sin(angle) * s_ref[...]

    def whole(*dims):
        return pl.BlockSpec(dims, lambda i, s: (0, 0))

    block = pl.BlockSpec((count, lanes), lambda i, s: (i, 0))
    return pl.pallas_call(
        body,
        grid_spec=pltpu.PrefetchScalarGridSpec(
            num_scalar_prefetch=1,
            grid=(8,),
            in_specs=[pl.BlockSpec(small.shape, lambda i, s: (0, 0, 0)), whole(1, lanes), whole(1, lanes)],
            out_specs=[
                whole(8, width),
                whole(1, width),
                whole(1, 4 * unit),
                whole(1, 3 * HEAD),
                pl.BlockSpec((1, 1, count), lambda i, s: (i, 0, 0)),
                block,
                block,
            ],
            scratch_shapes=[pltpu.VMEM(small.shape, F32)],
        ),
        out_shape=[
            shape((8, width), F32),
            shape((1, width), F32),
            shape((1, 4 * unit), F32),
            shape((1, 3 * HEAD), F32),
            shape((8, 1, count), F32),
            shape((8 * count, lanes), F32),
            shape((8 * count, lanes), F32),
        ],
        compiler_params=pltpu.CompilerParams(vmem_limit_bytes=40 * 1024 * 1024),
        cost_estimate=pl.CostEstimate(flops=int(COST), bytes_accessed=1024, transcendentals=0),
    )(place, small, freq, sign)


def join(pieces):
    count, width = pieces[0].shape
    blocks = len(pieces)

    def body(*refs):
        ins, out, held, sems_in, sems_out = refs[:blocks], refs[blocks], *refs[blocks + 1 :]

        def copy_in(k):
            return pltpu.make_async_copy(ins[k], held.at[k], sems_in.at[k])

        def copy_out(k):
            return pltpu.make_async_copy(held.at[k], out.at[pl.ds(k * count, count)], sems_out.at[k])

        for k in range(blocks):
            copy_in(k).start()
        for k in range(blocks):
            copy_in(k).wait()
            copy_out(k).start()
        for k in range(blocks):
            copy_out(k).wait()

    some = pl.BlockSpec(memory_space=pl.ANY)
    return pl.pallas_call(
        body,
        grid=(1,),
        in_specs=[some] * blocks,
        out_specs=some,
        out_shape=shape((blocks * count, width), pieces[0].dtype),
        scratch_shapes=[pltpu.VMEM((blocks, count, width), pieces[0].dtype)] + [pltpu.SemaphoreType.DMA((blocks,))] * 2,
        compiler_params=pltpu.CompilerParams(vmem_limit_bytes=40 * 1024 * 1024),
        cost_estimate=pl.CostEstimate(flops=int(4 * COST), bytes_accessed=1024, transcendentals=0),
    )(*pieces)


def join_heads(pieces, mine):
    rows, width = pieces[0].shape

    def body(mine_ref, *refs):
        for k, (xr, zr) in enumerate([(0, 0), (0, 1), (1, 0), (1, 1)]):
            at = ((mine_ref[1] ^ xr) * 2 + (mine_ref[0] ^ zr)) * rows
            refs[4][pl.ds(pl.multiple_of(at, rows), rows), :] = refs[k][...]

    return call(
        body,
        (1,),
        [pl.BlockSpec((rows, width), lambda i, s: (0, 0))] * 4,
        pl.BlockSpec((4 * rows, width), lambda i, s: (0, 0)),
        shape((4 * rows, width), BF16),
        tuple(pieces),
        mine,
    )


def norms(halves, gains, count):
    tokens, width = halves[0].shape
    each = tokens // count
    blocks = 2 * each

    def body(v_ref, a_ref, b_ref, first_ref, second_ref, stats_ref, x_buf, first_buf, second_buf, sems_in, sems_first, sems_second):
        def copy_in(k):
            half = (a_ref, b_ref)[k // each]
            return pltpu.make_async_copy(half.at[pl.ds(k % each * count, count)], x_buf.at[k % 2], sems_in.at[k % 2])

        def copy_first(k):
            return pltpu.make_async_copy(first_buf.at[k % 2], first_ref.at[pl.ds(k * count, count)], sems_first.at[k % 2])

        def copy_second(k):
            return pltpu.make_async_copy(second_buf.at[k % 2], second_ref.at[pl.ds(k * count, count)], sems_second.at[k % 2])

        copy_in(0).start()
        for k in range(blocks):
            slot = k % 2
            copy_in(k).wait()
            if k + 1 < blocks:
                copy_in(k + 1).start()
            if k >= 2:
                copy_first(k - 2).wait()
                copy_second(k - 2).wait()
            value = x_buf[slot].astype(F32)
            mean = jnp.mean(value, axis=-1, keepdims=True)
            center = value - mean
            scale = lax.rsqrt(jnp.mean(center * center, axis=-1, keepdims=True) + EPS)
            xhat = center * scale
            first_buf[slot] = (xhat * v_ref[0:1, :] + v_ref[1:2, :]).astype(BF16)
            second_buf[slot] = (xhat * v_ref[2:3, :] + v_ref[3:4, :]).astype(BF16)
            lane = lax.broadcasted_iota(jnp.int32, (count, 128), 1)
            stats_ref[k * count : (k + 1) * count, :] = jnp.where(lane == 0, mean, scale)
            copy_first(k).start()
            copy_second(k).start()
        for k in (blocks - 2, blocks - 1):
            copy_first(k).wait()
            copy_second(k).wait()

    some = pl.BlockSpec(memory_space=pl.ANY)
    return pl.pallas_call(
        body,
        grid=(1,),
        in_specs=[pl.BlockSpec((8, width), lambda i: (0, 0)), some, some],
        out_specs=[some, some, pl.BlockSpec((2 * tokens, 128), lambda i: (0, 0))],
        out_shape=[shape((2 * tokens, width), BF16)] * 2 + [shape((2 * tokens, 128), F32)],
        scratch_shapes=[pltpu.VMEM((2, count, width), BF16)] * 3 + [pltpu.SemaphoreType.DMA((2,))] * 3,
        compiler_params=pltpu.CompilerParams(vmem_limit_bytes=40 * 1024 * 1024),
        cost_estimate=pl.CostEstimate(flops=int(12 * COST), bytes_accessed=1024, transcendentals=0),
    )(gains, *halves)


def feed_up(second, w_up, bias, tile=512):
    tokens, width = second.shape
    deep, hidden = w_up[0].shape

    def body(s_ref, *refs):
        b_ref, act_ref, slope_ref = refs[4:]
        up = b_ref[...]
        for k in range(4):
            up = up + jnp.dot(s_ref[:, k * deep : (k + 1) * deep], refs[k][...], preferred_element_type=F32)
        phi_sum = 0.5 * (1.0 + lax.erf(up * (0.5**0.5)))
        act_ref[...] = (up * phi_sum).astype(BF16)
        slope_ref[...] = phi_sum + up * jnp.exp(-0.5 * up * up) * 0.3989422804014327

    block = pl.BlockSpec((tile, hidden), lambda i: (i, 0))
    return call(
        body,
        (tokens // tile,),
        [pl.BlockSpec((tile, width), lambda i: (i, 0))]
        + [pl.BlockSpec((deep, hidden), lambda i: (0, 0))] * 4
        + [pl.BlockSpec((1, hidden), lambda i: (0, 0))],
        [block, block],
        [shape((tokens, hidden), BF16), shape((tokens, hidden), F32)],
        (second, *w_up, bias),
        us=16,
    )


def either(steps, first_half, tile, width):
    half = steps // 2

    def spec(low):
        return pl.BlockSpec((tile, width), lambda i: (jnp.minimum(i, half - 1) if low else jnp.maximum(i - half, 0), 0))

    return [spec(first_half), spec(not first_half)]


def join_units(pieces, mine):
    unit, width = pieces[0].shape

    def body(mine_ref, *refs):
        for k, (zr, xr) in enumerate([(0, 0), (0, 1), (1, 0), (1, 1)]):
            at = ((mine_ref[0] ^ zr) * 2 + (mine_ref[1] ^ xr)) * unit
            refs[4][pl.ds(pl.multiple_of(at, unit), unit), :] = refs[k][...]

    return call(
        body,
        (1,),
        [pl.BlockSpec(p.shape, lambda i, s: (0, 0)) for p in pieces],
        pl.BlockSpec((4 * unit, width), lambda i, s: (0, 0)),
        shape((4 * unit, width), BF16),
        tuple(pieces),
        mine,
        us=3,
    )


def feed_back(g, w_down, slope, tile=512):
    half, width = g[0].shape
    steps = 2 * half // tile
    hidden = slope.shape[1]

    def body(ga_ref, gb_ref, w_ref, slope_ref, d_ref, column_ref):
        step = pl.program_id(0)

        @pl.when(step == 0)
        def _():
            column_ref[...] = jnp.zeros_like(column_ref)

        def work(g_ref):
            d_act = lax.dot_general(g_ref[...], w_ref[...], ROWS, preferred_element_type=F32)
            d_up = (d_act * slope_ref[...]).astype(BF16)
            d_ref[...] = d_up
            column_ref[...] += jnp.sum(d_up.astype(F32), axis=0, keepdims=True)

        pl.when(step < steps // 2)(lambda: work(ga_ref))
        pl.when(step >= steps // 2)(lambda: work(gb_ref))

    block = pl.BlockSpec((tile, hidden), lambda i: (i, 0))
    return call(
        body,
        (steps,),
        either(steps, True, tile, width) + [pl.BlockSpec((hidden, width), lambda i: (0, 0)), block],
        [block, pl.BlockSpec((1, hidden), lambda i: (0, 0))],
        [shape((2 * half, hidden), BF16), shape((1, hidden), F32)],
        (*g, w_down, slope),
        us=14,
    )


def weight_grad(left, right, mine, source, us=13):
    tokens, width = left.shape
    wide = right[0].shape[1]
    tile = width // 4
    count = len(right)

    def body(mine_ref, l_ref, *refs):
        part = lax.dot_general(l_ref[: tokens // count], refs[0][...], FIRSTS, preferred_element_type=F32)
        if count == 2:
            part = part + lax.dot_general(l_ref[tokens // 2 :], refs[1][...], FIRSTS, preferred_element_type=F32)
        for k, out in enumerate(refs[count:]):

            @pl.when(pl.program_id(0) == k)
            def _():
                out[...] = part.astype(out.dtype)

    return call(
        body,
        (4,),
        [pl.BlockSpec((tokens, tile), lambda i, s: (0, source(i, s)))]
        + [pl.BlockSpec(r.shape, lambda i, s: (0, 0)) for r in right],
        [pl.BlockSpec((tile, wide), lambda i, s: (0, 0))] * 4,
        [shape((tile, wide), BF16)] * 2 + [shape((tile, wide), F32)] * 2,
        (left, *right),
        mine,
        us=us,
    )


def head_grad(mixed, g, mine):
    tokens, head = mixed.shape
    width = g[0].shape[1]

    def body(mine_ref, l_ref, ga_ref, gb_ref, sent_ref, kept_ref):
        part = lax.dot_general(l_ref[: tokens // 2], ga_ref[...], FIRSTS, preferred_element_type=F32)
        part = part + lax.dot_general(l_ref[tokens // 2 :], gb_ref[...], FIRSTS, preferred_element_type=F32)
        upper, lower = part[: head // 2], part[head // 2 :]
        own = mine_ref[1] == 0
        sent_ref[...] = jnp.where(own, lower, upper).astype(BF16)
        kept_ref[...] = jnp.where(own, upper, lower)

    return call(
        body,
        (2,),
        [pl.BlockSpec((tokens, head), lambda i, s: (0, 0))]
        + [pl.BlockSpec((tokens // 2, width // 2), lambda i, s: (0, i))] * 2,
        [pl.BlockSpec((head // 2, width // 2), lambda i, s: (0, i))] * 2,
        [shape((head // 2, width), BF16), shape((head // 2, width), F32)],
        (mixed, *g),
        mine,
        us=5,
    )


def fold_tokens(kept, got):
    count, width = kept.shape
    tile = count // 4

    def body(k_ref, *refs):
        first_ref, second_ref, stays_ref = refs[4:]
        step = pl.program_id(0)
        for j in range(4):

            @pl.when(step == 3 - j)
            def _():
                total = k_ref[...].astype(F32) + refs[j][...].astype(F32)
                out = (stays_ref, stays_ref, second_ref, first_ref)[j]
                out[...] = total.astype(out.dtype)

    fixed = pl.BlockSpec((tile, width), lambda i: (0, 0))
    return call(
        body,
        (4,),
        [pl.BlockSpec((tile, width), lambda i: (3 - i, 0))] + [fixed] * 4,
        [fixed, fixed, pl.BlockSpec((tile, width), lambda i: (jnp.minimum(3 - i, 1), 0))],
        [shape((tile, width), BF16)] * 2 + [shape((2 * tile, width), F32)],
        (kept,) + tuple(got),
        us=5,
    )


def add_half(kept, got, rows, at):
    width = kept.shape[1]

    def body(k_ref, g_ref, o_ref):
        o_ref[...] = (k_ref[...] + g_ref[...].astype(F32)).astype(BF16)

    fixed = pl.BlockSpec((rows, width), lambda i: (0, 0))
    return call(
        body, (1,), [pl.BlockSpec((rows, width), lambda i: (at, 0)), fixed], fixed, shape((rows, width), BF16), (kept, got)
    )


def attend(first, w_qkv, b_qkv, g, w_proj, cosine, sine, docs):
    tokens, width = first.shape
    rows, _, count = docs.shape
    deep = w_qkv[0].shape[0]
    lanes = cosine.shape[1]
    half = ROT // 2
    scale = HEAD ** (-0.5)

    def body(f_ref, w0_ref, w1_ref, w2_ref, w3_ref, b_ref, ga_ref, gb_ref, p_ref, cos_ref, sin_ref, row_ref, mixed_ref, d_qkv_ref, column_ref):
        step = pl.program_id(0)

        @pl.when(step == 0)
        def _():
            column_ref[...] = jnp.zeros_like(column_ref)

        def work(g_ref):
            cos, sin = cos_ref[...], sin_ref[...]
            lane = lax.broadcasted_iota(jnp.int32, cos.shape, 1)

            def turn(v, sign):
                front = v[:, :lanes]
                other = jnp.where(lane < half, pltpu.roll(front, lanes - half, 1), pltpu.roll(front, half, 1))
                return jnp.concatenate([front * cos + sign * (other * sin), v[:, lanes:]], axis=1)

            qkv = b_ref[...]
            for k, w_ref in enumerate((w0_ref, w1_ref, w2_ref, w3_ref)):
                qkv = qkv + jnp.dot(f_ref[:, k * deep : (k + 1) * deep], w_ref[...], preferred_element_type=F32)
            d_mixed = lax.dot_general(g_ref[...], p_ref[...], ROWS, preferred_element_type=F32).astype(BF16)
            rq = turn(qkv[:, :HEAD], 1.0).astype(BF16)
            rk = turn(qkv[:, HEAD : 2 * HEAD], 1.0).astype(BF16)
            rv = qkv[:, 2 * HEAD :].astype(BF16)
            here = lax.broadcasted_iota(jnp.int32, (count, count), 0)
            there = lax.broadcasted_iota(jnp.int32, (count, count), 1)
            across = jnp.broadcast_to(row_ref[0], (count, count))
            allowed = (across == across.T) & (there <= here)
            raw = lax.dot_general(rq, rk, ROWS, preferred_element_type=F32)
            scores = jnp.where(allowed, raw * scale, MASKED)
            expo = jnp.exp(scores - jnp.max(scores, axis=1, keepdims=True))
            probs = expo / jnp.sum(expo, axis=1, keepdims=True)
            weights = probs.astype(BF16)
            mixed_ref[...] = jnp.dot(weights, rv, preferred_element_type=F32).astype(BF16)
            d_prob = lax.dot_general(d_mixed, rv, ROWS, preferred_element_type=F32)
            d_score = probs * (d_prob - jnp.sum(probs * d_prob, axis=1, keepdims=True))
            d_raw = (d_score * scale).astype(BF16)
            d_rq = jnp.dot(d_raw, rk, preferred_element_type=F32)
            d_rk = lax.dot_general(d_raw, rq, FIRSTS, preferred_element_type=F32)
            d_rv = lax.dot_general(weights, d_mixed, FIRSTS, preferred_element_type=F32)
            d_qkv = jnp.concatenate([turn(d_rq, -1.0), turn(d_rk, -1.0), d_rv], axis=1).astype(BF16)
            d_qkv_ref[...] = d_qkv
            column_ref[...] += jnp.sum(d_qkv.astype(F32), axis=0, keepdims=True)

        pl.when(step < rows // 2)(lambda: work(ga_ref))
        pl.when(step >= rows // 2)(lambda: work(gb_ref))

    def row(*dims):
        return pl.BlockSpec(dims, lambda i: (i, 0))

    def whole(*dims):
        return pl.BlockSpec(dims, lambda i: (0, 0))

    return call(
        body,
        (rows,),
        [
            row(count, width),
            *([whole(deep, 3 * HEAD)] * 4),
            whole(1, 3 * HEAD),
            *either(rows, True, count, width),
            whole(HEAD, width),
            row(count, lanes),
            row(count, lanes),
            pl.BlockSpec((1, 1, count), lambda i: (i, 0, 0)),
        ],
        [row(count, HEAD), row(count, 3 * HEAD), whole(1, 3 * HEAD)],
        [shape((tokens, HEAD), BF16), shape((tokens, 3 * HEAD), BF16), shape((1, 3 * HEAD), F32)],
        (first, *w_qkv, b_qkv, *g, w_proj, cosine, sine, docs),
        us=17,
    )


def branch_sum(act, w_down, mixed, w_proj, tile=512, block=256):
    tokens, hidden = act.shape
    width = w_down.shape[1]
    steps = tokens // tile
    sent = steps // 2
    each = tile // block
    blocks = sent * each

    def body(a_ref, w_ref, m_ref, p_ref, *outs):
        part = jnp.dot(a_ref[...], w_ref[...], preferred_element_type=F32)
        part = (part + jnp.dot(m_ref[...], p_ref[...], preferred_element_type=F32)).astype(BF16)
        outs[blocks][...] = part
        step = pl.program_id(0)
        for k in range(sent):

            @pl.when(step == k)
            def _():
                for j in range(each):
                    outs[k * each + j][...] = part[j * block : (j + 1) * block]

    def turned(i):
        return (lax.rem(i + sent, steps), 0)

    fixed = pl.BlockSpec((block, width), lambda i: (0, 0))
    return call(
        body,
        (steps,),
        [
            pl.BlockSpec((tile, hidden), turned),
            pl.BlockSpec((hidden, width), lambda i: (0, 0)),
            pl.BlockSpec((tile, HEAD), turned),
            pl.BlockSpec((HEAD, width), lambda i: (0, 0)),
        ],
        [fixed] * blocks + [pl.BlockSpec((tile, width), lambda i: (jnp.maximum(i - sent, 0), 0))],
        [shape((block, width), BF16)] * blocks + [shape((tokens // 2, width), BF16)],
        (act, w_down, mixed, w_proj),
        us=16,
    )


def edge_sum(d_up, w_up, d_qkv, w_qkv, x, stats, gains, tile=256):
    tokens, hidden = d_up.shape
    deep = w_up[0].shape[0]
    width = 4 * deep
    steps = tokens // tile
    sent = steps // 2

    def body(du_ref, dq_ref, xa_ref, xb_ref, stats_ref, v_ref, *refs):
        outs = refs[8:]
        sums_ref = outs[sent + 1]
        step = pl.program_id(0)

        @pl.when(step == 0)
        def _():
            sums_ref[...] = jnp.zeros_like(sums_ref)

        for k in range(4):
            part = slice(k * deep, (k + 1) * deep)
            d_second = lax.dot_general(du_ref[...], refs[k][...], ROWS, preferred_element_type=F32)
            d_first = lax.dot_general(dq_ref[...], refs[4 + k][...], ROWS, preferred_element_type=F32)
            x = jnp.where(step < sent, xb_ref[:, part], xa_ref[:, part])
            xhat = (x.astype(F32) - stats_ref[:, 0:1]) * stats_ref[:, 1:2]
            outs[sent][:, part] = (d_first * v_ref[0:1, part] + d_second * v_ref[2:3, part]).astype(BF16)
            sums_ref[0:1, part] += jnp.sum(d_first * xhat, axis=0, keepdims=True)
            sums_ref[1:2, part] += jnp.sum(d_first, axis=0, keepdims=True)
            sums_ref[2:3, part] += jnp.sum(d_second * xhat, axis=0, keepdims=True)
            sums_ref[3:4, part] += jnp.sum(d_second, axis=0, keepdims=True)

        for j in range(sent):

            @pl.when(step == j)
            def _():
                outs[j][...] = outs[sent][...]

    def turned(i):
        return (lax.rem(i + sent, steps), 0)

    def whole(*dims):
        return pl.BlockSpec(dims, lambda i: (0, 0))

    return call(
        body,
        (steps,),
        [
            pl.BlockSpec((tile, hidden), turned),
            pl.BlockSpec((tile, 3 * HEAD), turned),
            *either(steps, False, tile, width),
            pl.BlockSpec((tile, 128), turned),
            whole(8, width),
        ]
        + [whole(deep, hidden)] * 4
        + [whole(deep, 3 * HEAD)] * 4,
        [whole(tile, width)] * sent
        + [pl.BlockSpec((tile, width), lambda i: (jnp.maximum(i - sent, 0), 0)), whole(8, width)],
        [shape((tile, width), BF16)] * sent + [shape((tokens // 2, width), BF16), shape((8, width), F32)],
        (d_up, d_qkv, *x, stats, gains, *w_up, *w_qkv),
        us=28,
        limit=48,
    )


def total(parts, rows):
    width = parts[0].shape[1]

    def body(*refs):
        value = refs[0][...].astype(F32)
        for ref in refs[1:-1]:
            value = value + ref[...].astype(F32)
        refs[-1][...] = value

    return call(
        body,
        (1,),
        [pl.BlockSpec((min(rows, p.shape[0]), width), lambda i: (0, 0)) for p in parts],
        pl.BlockSpec((rows, width), lambda i: (0, 0)),
        shape((rows, width), F32),
        tuple(parts),
        us=3,
    )


def finish(edge_k, edge_g0, edge_got, x0, g, mine):
    count, width = x0.shape
    wide = width // 16

    def body(mine_ref, k_ref, a_ref, b_ref, x_ref, g_ref, o_ref):
        edge = k_ref[...] + a_ref[...].astype(F32) + b_ref[...].astype(F32)
        value = x_ref[...].astype(F32)
        center = value - jnp.mean(value, axis=-1, keepdims=True)
        scale = lax.rsqrt(jnp.mean(center * center, axis=-1, keepdims=True) + EPS)
        xhat = center * scale
        back = edge - jnp.mean(edge, axis=-1, keepdims=True) - xhat * jnp.mean(edge * xhat, axis=-1, keepdims=True)
        back = back * scale
        for j in range(16):
            xr, zr, b, c = bits_of(j, 4)
            source = (zr ^ mine_ref[0]) * 8 + b * 4 + c * 2 + (xr ^ mine_ref[1])
            place = pl.ds(pl.multiple_of(source * wide, wide), wide)
            o_ref[:, place] = g_ref[:, place].astype(F32) + back[:, j * wide : (j + 1) * wide]

    tile = count // 2
    block = pl.BlockSpec((tile, width), lambda i, s: (i, 0))
    return call(
        body, (2,), [block] * 5, block, shape((count, width), F32), (edge_k, edge_g0, edge_got, x0, g), mine, us=5
    )


def local_tuned(
    inputs,
    doc_ids,
    attn_gain,
    attn_shift,
    ffn_gain,
    ffn_shift,
    qkv_weight,
    qkv_bias,
    proj_weight,
    proj_bias,
    up_weight,
    up_bias,
    down_weight,
    down_bias,
    cotangent,
):
    n = lax.axis_size(AXIS)
    lay = Layout(n)
    count, width = inputs.shape
    rows = width // n
    unit = up_bias.shape[0]
    hidden = 4 * unit
    me = lax.axis_index(AXIS)
    mzh, mx = lay.mine(ZH), lay.mine(X)
    mine = jnp.stack([mzh, mx]).astype(jnp.int32)

    cols = split_columns(up_weight, qkv_weight)
    (x0,) = after((inputs,), cols)
    x0 = order_columns(x0, mine)
    down_z = flip(down_weight, ZH)
    down_x = flip(down_weight, X)
    cols = lay.to_columns(cols)
    x1 = flip(x0, ZL)
    x2 = flip(x0, Y)
    g2 = flip(cotangent, Y)
    small = jnp.concatenate(
        [doc_ids[0].astype(BF16), up_bias, attn_gain, attn_shift, ffn_gain, ffn_shift, proj_bias, down_bias, qkv_bias]
    )
    small = jnp.pad(small, (0, 16 * 128 - small.shape[0])).reshape(16, 128)
    small = jnp.broadcast_to(small[None], (n, 16, 128))

    cols, down_z, down_x, x1, x2, g2, small, g0 = after((cols, down_z, down_x, x1, x2, g2, small, cotangent))
    up_cols, qkv_cols = cols[:, :, :hidden], cols[:, :, hidden:]
    small = lax.all_to_all(small, AXIS, split_axis=0, concat_axis=0, tiled=True)
    up_z = flip(up_cols, ZH)
    up_x = flip(up_cols, X)
    g1 = flip(g0, ZL)
    x3 = flip(x1, Y)
    down_xz = flip(down_z, X)

    freq = 10000.0 ** (-2.0 * np.arange(ROT // 2, dtype=np.float32) / ROT)
    rest = np.zeros(128 - ROT, np.float32)
    freq = jnp.asarray(np.concatenate([freq, freq, rest])[None], F32)
    sign = jnp.asarray(np.concatenate([np.full(ROT // 2, -1.0), np.full(ROT // 2, 1.0), rest])[None], F32)
    bit_of = jnp.stack([lay.mine(b) for b in (ZH, X, ZL, Y, CORE)] + [me]).astype(jnp.int32)
    here = lay.mine(ZL) * 4 + lay.mine(Y) * 2 + lay.mine(CORE)

    def restore(v):
        v = v.reshape(v.shape[0], 2, 2, 4, 2 * rows).transpose(0, 2, 3, 1, 4)
        v = jnp.where(mzh == 1, v[:, ::-1], v)
        v = jnp.where(mx == 1, v[:, :, :, ::-1], v)
        return v.reshape(v.shape[0], width)

    up_z, up_x, x1, x2, x3, g1, down_xz, small, qkv_cols, proj0 = after(
        (up_z, up_x, x1, x2, x3, g1, down_xz, small, qkv_cols, proj_weight)
    )
    gains, b_out, b_up, b_qkv, docs, cosine, sine = prepare(small, bit_of, freq, sign, rows, unit, count)
    xa = join([x0, x1, x2, x3])
    xb = flip(xa, CORE)
    up_xz = flip(up_z, X)
    g3 = flip(g1, Y)
    proj0 = lay.exchange_heads(proj0)
    w_down = join_units([down_weight, down_x, down_z, down_xz], mine)
    gains, g0, g1, g2, g3, qkv_cols, proj0, up_xz, xb, w_down = after(
        (gains, g0, g1, g2, g3, qkv_cols, proj0, up_xz, xb, w_down)
    )
    ga = join([g0, g1, g2, g3])
    gb = flip(ga, CORE)
    qkv_z = flip(qkv_cols, ZH)
    qkv_x = flip(qkv_cols, X)
    proj_z = flip(proj0, ZH)
    proj_x = flip(proj0, X)
    first, second, stats = norms([xa, xb], gains, count)
    w_up = [v.reshape(-1, hidden) for v in (up_cols, up_z, up_x, up_xz)]
    act, slope = feed_up(second, w_up, b_up)
    act, qkv_z, qkv_x, proj_x, gb = after((act, qkv_z, qkv_x, proj_x, gb))
    g = [ga, gb]
    x = [xa, xb]
    qkv_xz = flip(qkv_z, X)

    def hidden_block(step, s):
        return (s[0] ^ (1 - lax.rem(step, 2))) * 2 + (s[1] ^ jnp.where(step < 2, 1, 0))

    def feature_block(step, s):
        return 3 - step

    down_s1, down_s0, down_k1, down_k0 = weight_grad(act, g, mine, hidden_block, us=15)
    down_g1 = flip(down_s1, X)
    slope, qkv_xz, down_k1, proj_z = after((slope, qkv_xz, down_k1, proj_z))
    proj_xz = flip(proj_z, X)
    d_up, column_up = feed_back(g, w_down, slope)
    d_up, down_s0 = after((d_up, down_s0))
    down_g0 = flip(down_s0, X)
    up_s1, up_s0, up_k1, up_k0 = weight_grad(second, [d_up], mine, feature_block, us=12)
    up_g1 = flip(up_s1, X)

    down_g1, up_k1, proj_xz = after((down_g1, up_k1, proj_xz))
    down_sent = add_half(down_k1, down_g1, unit, 0)
    down_got = flip(down_sent, ZH)
    w_proj = join_heads([proj0, proj_z, proj_x, proj_xz], mine)
    w_qkv = [v.reshape(-1, 3 * HEAD) for v in (qkv_cols, qkv_z, qkv_x, qkv_xz)]
    (first_,) = after((first,), down_sent)
    mixed, d_qkv, column_qkv = attend(first_, w_qkv, b_qkv, g, w_proj, cosine, sine, docs)
    act, mixed, d_qkv, down_g0 = after((act, mixed, d_qkv, down_g0))
    *out_s, out_k = branch_sum(act, w_down, mixed, w_proj)
    out_g = [flip(v, CORE) for v in out_s]
    d_qkv, out_k, up_g1, up_s0, down_got = after((d_qkv, out_k, up_g1, up_s0, down_got))
    up_g0 = flip(up_s0, X)
    up_sent = add_half(up_k1, up_g1, up_k1.shape[0], 0)
    up_got = flip(up_sent, ZH)
    *out_g, out_k = after((*out_g, out_k), up_sent)
    out_s1, out_s0, out_k = fold_tokens(out_k, out_g)
    out_g1 = flip(out_s1, Y)
    out_g0 = flip(out_s0, Y)
    d_qkv, out_k = after((d_qkv, out_k))
    qkv_s1, qkv_s0, qkv_k1, qkv_k0 = weight_grad(first, [d_qkv], mine, feature_block, us=10)
    qkv_g1 = flip(qkv_s1, X)
    mixed, qkv_k1 = after((mixed, qkv_k1))
    proj_s, proj_k = head_grad(mixed, g, mine)
    out_g1, out_k, up_g0, proj_s, qkv_s0 = after((out_g1, out_k, up_g0, proj_s, qkv_s0))
    qkv_g0 = flip(qkv_s0, X)
    proj_g = flip(proj_s, X)
    out_sent = add_half(out_k, out_g1, count, 1)
    out_got = flip(out_sent, ZL)

    d_up, d_qkv = after((d_up, d_qkv), out_sent)
    *edge_s, edge_k, sums = edge_sum(d_up, w_up, d_qkv, w_qkv, x, stats, gains)

    *edge_s, edge_k, qkv_g1, up_got, out_g0, sums = after((*edge_s, edge_k, qkv_g1, up_got, out_g0, sums))
    edge_g = [flip(v, CORE) for v in edge_s]
    qkv_sent = add_half(qkv_k1, qkv_g1, qkv_k1.shape[0], 0)
    qkv_got = flip(qkv_sent, ZH)
    up_got, edge_k = after((up_got, edge_k), qkv_sent)
    up_sum = (up_k0 + up_g0.astype(F32) + up_got.astype(F32)).astype(BF16)
    up_back = lay.to_columns(up_sum.reshape(8, rows, hidden))
    edge_k, up_sum, out_got = after((edge_k, up_sum, out_got))
    *edge_g, edge_k = after((*edge_g, edge_k))
    edge_s1, edge_s0, edge_k = fold_tokens(edge_k, edge_g)
    edge_g1 = flip(edge_s1, Y)

    edge_k, sums, column_up, column_qkv = after((edge_k, sums, column_up, column_qkv))
    column_out = jnp.sum(cotangent.astype(F32), axis=0)
    spread_up = lax.dynamic_update_slice(jnp.zeros((HEADS, hidden), F32), column_up, (here, 0))
    spread_up = spread_up.reshape(2, 2, 2, 2, 2, unit).transpose(3, 0, 1, 4, 2, 5)
    spread_qkv = lax.dynamic_update_slice(jnp.zeros((HEADS, 3 * HEAD), F32), column_qkv, (here, 0))
    spread_qkv = spread_qkv.reshape(2, 2, 2, 3, HEAD).transpose(3, 2, 0, 1, 4)
    sums = restore(sums[:4])
    flat = [v.reshape(n, -1) for v in (sums[0], sums[1], sums[2], sums[3], column_out, spread_qkv, spread_up)]
    flat = jnp.concatenate(flat, axis=1)
    flat, up_back = after((flat, up_back))
    sums = lax.all_to_all(flat, AXIS, split_axis=0, concat_axis=0, tiled=True)
    qkv_got, qkv_g0, sums, proj_g, edge_k = after((qkv_got, qkv_g0, sums, proj_g, edge_k))
    qkv_sum = (qkv_k0 + qkv_g0.astype(F32) + qkv_got.astype(F32)).astype(BF16)
    qkv_back = lay.to_columns(qkv_sum.reshape(8, rows, 3 * HEAD))
    proj_sum = (proj_k + proj_g.astype(F32)).reshape(2, rows, width)
    proj_kept = lax.dynamic_index_in_dim(proj_sum, mzh, 0, keepdims=False)
    proj_sent = lax.dynamic_index_in_dim(proj_sum, 1 - mzh, 0, keepdims=False).astype(BF16)
    proj_got = flip(proj_sent, ZH)
    edge_g1, edge_s0, qkv_sum, proj_sent = after((edge_g1, edge_s0, qkv_sum, proj_sent))
    edge_g0 = flip(edge_s0, Y)
    edge_sent = add_half(edge_k, edge_g1, count, 1)
    edge_got = flip(edge_sent, ZL)
    qkv_back, up_back, out_k, down_k0 = after((qkv_back, up_back, out_k, down_k0), edge_sent)
    grad_up = join_up(up_back)
    grad_qkv = join_qkv(qkv_back)
    layer_out = total([inputs, b_out, out_k, out_g0, out_got], count)
    grad_down = total([down_k0, down_g0, down_got], unit)
    proj_got, edge_k, layer_out, grad_down = after((proj_got, edge_k, layer_out, grad_down))
    proj_back = lay.exchange_heads((proj_kept + proj_got.astype(F32)).astype(BF16))
    edge_got, edge_g0, edge_k = after((edge_got, edge_g0, edge_k))
    grad_inputs = finish(edge_k, edge_g0, edge_got, x0, cotangent, mine)
    proj_back, grad_inputs = after((proj_back, grad_inputs))
    grad_proj = proj_back.astype(F32)
    sums = jnp.sum(sums, axis=0)
    got, at = [], 0
    for size in [rows] * 5 + [3 * rows, unit]:
        got.append(sums[at : at + size])
        at += size
    return (
        layer_out,
        grad_inputs,
        got[0],
        got[1],
        got[2],
        got[3],
        grad_qkv,
        got[5],
        grad_proj,
        got[4],
        grad_up,
        got[6],
        grad_down,
        got[4],
    )


def solution(mesh):
    tokens, rows = P(AXIS, None), P(AXIS)
    return jax.shard_map(
        local_tuned if mesh.shape[AXIS] == 32 else local_any,
        mesh=mesh,
        in_specs=(tokens, tokens, rows, rows, rows, rows, tokens, rows, tokens, rows, tokens, rows, tokens, rows, tokens),
        out_specs=(tokens, tokens, rows, rows, rows, rows, tokens, rows, tokens, rows, tokens, rows, tokens, rows),
        check_vma=False,
    )
```

profile of v0, /device:TPU:0, one launch (start us, length us, event | category | flops | bytes accessed | tf_op | source)
XLA Modules:
  0.0 487.1 jit_solution(16076498628572175835)
XLA Ops:
  4.5 5.4 %all-to-all-start = ((bf16[8,64,1792]{2,1,0:T(8,128)(2,1)}), bf16[8,64,1792]{2,1,0:T(8,128)(2,1)}, u32[]{:S(2)}, u32[]{:S(2)}) async-start(bf16[8,64,1792]{2,1,0:T(8,128)(2,1)} %copy-done.9), calls=%async_computation | async-start | bytes 3670016 | tf_op jit(solution)/shard_map/all_to_all | solution.py:185
  14.4 3.0 collective-permute-start
  19.6 58.3 %collective-permute-done.2.refs_1_ = bf16[256,2048]{1,0:T(8,128)(2,1)} collective-permute-done((bf16[256,2048]{1,0:T(8,128)(2,1)S(1)}, bf16[256,2048]{1,0:T(8,128)(2,1)}, u32[]{:S(2)}, u32[]{:S(2)}) %collective-permute-start.2) | collective-permute-done | bytes 1048608 | tf_op jit(solution)/shard_map/ppermute | solution.py:383
  88.0 3.5 all-to-all-start.1
  93.6 41.5 %all-to-all-done.1.small_ref = bf16[32,16,128]{2,1,0:T(8,128)(2,1)S(1)} async-done(((bf16[32,16,128]{2,1,0:T(8,128)(2,1)}), bf16[32,16,128]{2,1,0:T(8,128)(2,1)S(1)}, u32[]{:S(2)}, u32[]{:S(2)}) %all-to-all-start.1) | async-done | bytes 131104 | tf_op jit(solution)/shard_map/all_to_all | solution.py:1142
  135.1 3.5 shard_map.275.a_ref.xa_ref
  143.7 6.0 %shard_map.274 = (f32[8,2048]{1,0:T(8,128)S(1)}, f32[1,2048]{1,0:T(1,128)S(1)}, f32[1,1024]{1,0:T(1,128)S(1)}, f32[1,768]{1,0:T(1,128)S(1)}, f32[8,1,256]{2,1,0:...) custom-call(s32[6]{0:T(128)S(1)} %stack.33.place_ref, bf16[32,16,128]{2,1,0:T(8,128)(2,1)S(1)} %all-to-all-done.1.small_ref, ...), custom_call_target="tpu_custom_call" | custom-call | flops 450000000 | bytes 1024 | tf_op jit(solution)/shard_map/pallas_call | solution.py:553
  158.5 6.1 %collective-permute-done.10.refs_3_ = bf16[256,2048]{1,0:T(8,128)(2,1)} collective-permute-done((bf16[256,2048]{1,0:T(8,128)(2,1)}, bf16[256,2048]{1,0:T(8,128)(2,1)}, u32[]{:S(2)}, u32[]{:S(2)}) %collective-permute-start.10) | collective-permute-done | bytes 1048608 | tf_op jit(solution)/shard_map/ppermute | solution.py:383
  170.5 13.6 %shard_map.277 = (bf16[2048,2048]{1,0:T(8,128)(2,1)}, bf16[2048,2048]{1,0:T(8,128)(2,1)}, f32[2048,128]{1,0:T(8,128)S(1)}) custom-call(f32[8,2048]{1,0:T(8,128)S(1)} %get-tuple-element.194.v_ref, bf16[1024,2048]{1,0:T(8,128)(2,1)} %shard_map.275.a_ref.xa_ref, bf16[1024,2048]{1,0:T(8,128)(2,1)} %collective-permute-done.13.b_ref.xb_ref), custom_call_target="tpu_custom_call" | custom-call | flops 5400000000 | bytes 1024 | tf_op jit(solution)/shard_map/pallas_call | solution.py:678
  185.1 16.2 %shard_map.278 = (bf16[2048,1024]{1,0:T(8,128)(2,1)S(1)}, f32[2048,1024]{1,0:T(8,128)}) custom-call(bf16[2048,2048]{1,0:T(8,128)(2,1)} %get-tuple-element.196.s_ref.l_ref, bf16[512,1024]{1,0:T(8,128)(2,1)} %bitcast.7.refs_0_, bf16[512,1024]{1,0:T(8,128)(2,1)} %bitcast.8.refs_1_, bf16[512,1024]{1,0:T(8,128)(2,1)} %bitcast.9.refs_2_, ...), custom_call_target="tpu_custom_call" | custom-call | flops 7200000000 | bytes 1024 | tf_op jit(solution)/shard_map/pallas_call | solution.py:394
  201.4 3.5 collective-permute-done.14
  208.3 14.7 %shard_map.280 = (bf16[256,2048]{1,0:T(8,128)(2,1)S(1)}, bf16[256,2048]{1,0:T(8,128)(2,1)S(1)}, f32[256,2048]{1,0:T(8,128)S(1)}, f32[256,2048]{1,0:T(8,128)S(1)}) custom-call(s32[2]{0:T(128)S(1)} %pad_add_fusion.mine_ref, bf16[2048,1024]{1,0:T(8,128)(2,1)S(1)} %get-tuple-element.237.l_ref.a_ref, bf16[1024,2048]{1,0:T(8,128)(2,1)} %copy-done, ...), custom_call_target="tpu_custom_call" | custom-call | flops 6750000128 | bytes 1024 | tf_op jit(solution)/shard_map/pallas_call | solution.py:396
  230.8 12.5 %shard_map.281 = (bf16[2048,1024]{1,0:T(8,128)(2,1)S(1)}, f32[1,1024]{1,0:T(1,128)S(1)}) custom-call(bf16[1024,2048]{1,0:T(8,128)(2,1)S(1)} %copy-done.1, bf16[1024,2048]{1,0:T(8,128)(2,1)S(1)} %copy-done.11, bf16[1024,2048]{1,0:T(8,128)(2,1)} %copy-done.13, f32[2048,1024]{1,0:T(8,128)} %get-tuple-element.216.slope_ref), custom_call_target="tpu_custom_call" | custom-call | flops 6300000256 | bytes 1024 | tf_op jit(solution)/shard_map/pallas_call | solution.py:394
  249.6 13.0 %shard_map.282 = (bf16[512,1024]{1,0:T(8,128)(2,1)S(1)}, bf16[512,1024]{1,0:T(8,128)(2,1)}, f32[512,1024]{1,0:T(8,128)S(1)}, f32[512,1024]{1,0:T(8,128)S(1)}) custom-call(s32[2]{0:T(128)S(1)} %pad_add_fusion.mine_ref, bf16[2048,2048]{1,0:T(8,128)(2,1)} %get-tuple-element.196.s_ref.l_ref, bf16[2048,1024]{1,0:T(8,128)(2,1)S(1)} %copy-done.57), custom_call_target="tpu_custom_call" | custom-call | flops 5400000000 | bytes 1024 | tf_op jit(solution)/shard_map/pallas_call | solution.py:396
  267.0 17.8 %shard_map.285 = (bf16[2048,256]{1,0:T(8,128)(2,1)S(1)}, bf16[2048,768]{1,0:T(8,128)(2,1)S(1)}, f32[1,768]{1,0:T(1,128)S(1)}) custom-call(bf16[2048,2048]{1,0:T(8,128)(2,1)} %get-tuple-element.223.f_ref.l_ref, bf16[512,768]{1,0:T(8,128)(2,1)S(1)} %bitcast.34, bf16[512,768]{1,0:T(8,128)(2,1)S(1)} %bitcast.36, bf16[512,768]{1,0:T(8,128)(2,1)S(1)} %bitcast.38, ...), custom_call_target="tpu_custom_call" | custom-call | flops 7649999872 | bytes 1024 | tf_op jit(solution)/shard_map/pallas_call | solution.py:394
  286.5 15.2 %shard_map.286 = (bf16[256,2048]{1,0:T(8,128)(2,1)S(1)}, bf16[256,2048]{1,0:T(8,128)(2,1)S(1)}, bf16[256,2048]{1,0:T(8,128)(2,1)S(1)}, bf16[256,2048]{1,0:T(8,128)(2,1)S(1)}, bf16[1024,2048]{1,0:T(8,128)(2,1)S(1)}) custom-call(bf16[2048,1024]{1,0:T(8,128)(2,1)} %copy-done.66, bf16[1024,2048]{1,0:T(8,128)(2,1)} %copy-done.13, ...), custom_call_target="tpu_custom_call" | custom-call | flops 7200000000 | bytes 1024 | tf_op jit(solution)/shard_map/pallas_call | solution.py:394
  304.7 6.5 %collective-permute-done.24.refs_2_ = bf16[256,2048]{1,0:T(8,128)(2,1)S(1)} collective-permute-done((bf16[256,2048]{1,0:T(8,128)(2,1)S(1)}, bf16[256,2048]{1,0:T(8,128)(2,1)S(1)}, u32[]{:S(2)}, u32[]{:S(2)}) %collective-permute-start.24) | collective-permute-done | bytes 1048608 | tf_op jit(solution)/shard_map/ppermute | solution.py:383
  313.1 4.3 shard_map.288
  321.8 11.1 %shard_map.289 = (bf16[512,768]{1,0:T(8,128)(2,1)}, bf16[512,768]{1,0:T(8,128)(2,1)S(1)}, f32[512,768]{1,0:T(8,128)S(1)}, f32[512,768]{1,0:T(8,128)S(1)}) custom-call(s32[2]{0:T(128)S(1)} %pad_add_fusion.mine_ref, bf16[2048,2048]{1,0:T(8,128)(2,1)} %get-tuple-element.223.f_ref.l_ref, bf16[2048,768]{1,0:T(8,128)(2,1)S(1)} %copy-done.63), custom_call_target="tpu_custom_call" | custom-call | flops 4499999744 | bytes 1024 | tf_op jit(solution)/shard_map/pallas_call | solution.py:396
  338.2 3.8 shard_map.290
  347.5 27.1 %shard_map.292 = (bf16[256,2048]{1,0:T(8,128)(2,1)}, bf16[256,2048]{1,0:T(8,128)(2,1)}, bf16[256,2048]{1,0:T(8,128)(2,1)}, bf16[256,2048]{1,0:T(8,128)(2,1)}, bf...) custom-call(bf16[2048,1024]{1,0:T(8,128)(2,1)} %copy-done.56, bf16[2048,768]{1,0:T(8,128)(2,1)} %copy-done.62, ...), custom_call_target="tpu_custom_call" | custom-call | flops 12600000512 | bytes 1024 | tf_op jit(solution)/shard_map/pallas_call | solution.py:394
  376.0 3.1 add_convert_fusion
  379.1 3.8 all-to-all-start.2
  383.2 6.5 %collective-permute-done.40.refs_4_ = bf16[256,2048]{1,0:T(8,128)(2,1)} collective-permute-done((bf16[256,2048]{1,0:T(8,128)(2,1)}, bf16[256,2048]{1,0:T(8,128)(2,1)}, u32[]{:S(2)}, u32[]{:S(2)}) %collective-permute-start.40) | collective-permute-done | bytes 1048608 | tf_op jit(solution)/shard_map/ppermute | solution.py:383
  391.8 5.6 %shard_map.294 = (bf16[256,2048]{1,0:T(8,128)(2,1)S(1)}, bf16[256,2048]{1,0:T(8,128)(2,1)}, f32[512,2048]{1,0:T(8,128)S(1)}) custom-call(bf16[1024,2048]{1,0:T(8,128)(2,1)} %get-tuple-element.291.k_ref, bf16[256,2048]{1,0:T(8,128)(2,1)} %collective-permute-done.36.refs_0_, bf16[256,2048]{1,0:T(8,128)(2,1)} %collective-permute-done.37.refs_1_, ...), custom_call_target="tpu_custom_call" | custom-call | flops 2249999872 | bytes 1024 | tf_op jit(solution)/shard_map/pallas_call | solution.py:394
  401.4 5.4 %all-to-all-done.2.p_ref = bf16[8,64,1024]{2,1,0:T(8,128)(2,1)S(1)} async-done(((bf16[8,64,1024]{2,1,0:T(8,128)(2,1)}), bf16[8,64,1024]{2,1,0:T(8,128)(2,1)S(1)}, u32[]{:S(2)}, u32[]{:S(2)}) %all-to-all-start.2) | async-done | bytes 1048608 | tf_op jit(solution)/shard_map/all_to_all | solution.py:185
  412.3 18.1 %all-to-all-done.3 = f32[32,1,768]{2,1,0:T(1,128)S(1)} async-done(((f32[32,1,768]{2,1,0:T(1,128)}), f32[32,1,768]{2,1,0:T(1,128)S(1)}, u32[]{:S(2)}, u32[]{:S(2)}) %all-to-all-start.3) | async-done | bytes 98336 | tf_op jit(solution)/shard_map/all_to_all | solution.py:1259
  430.5 3.0 add_convert_fusion.1
  433.4 4.2 all-to-all-start.4
  457.8 3.1 shard_map.296
  460.9 14.3 %collective-permute-done.42 = bf16[64,2048]{1,0:T(8,128)(2,1)} collective-permute-done((bf16[64,2048]{1,0:T(8,128)(2,1)S(1)}, bf16[64,2048]{1,0:T(8,128)(2,1)}, u32[]{:S(2)}, u32[]{:S(2)}) %collective-permute-start.42) | collective-permute-done | bytes 262176 | tf_op jit(solution)/shard_map/ppermute | solution.py:383
  480.9 4.6 shard_map.298
  (314 shorter events, 127.1 us)
Async XLA Ops:
  4.5 73.4 %all-to-all-start = ((bf16[8,64,1792]{2,1,0:T(8,128)(2,1)}), bf16[8,64,1792]{2,1,0:T(8,128)(2,1)}, u32[]{:S(2)}, u32[]{:S(2)}) async-start(bf16[8,64,1792]{2,1,0:T(8,128)(2,1)} %copy-done.9), calls=%async_computation | async-start | bytes 3670016 | tf_op jit(solution)/shard_map/all_to_all | solution.py:185
  10.8 67.1 %collective-permute-start.2 = (bf16[256,2048]{1,0:T(8,128)(2,1)S(1)}, bf16[256,2048]{1,0:T(8,128)(2,1)}, u32[]{:S(2)}, u32[]{:S(2)}) collective-permute-start(bf16[256,2048]{1,0:T(8,128)(2,1)S(1)} %shard_map.273.refs_0_.x_ref), channel_id=1, source_target_pairs={{0,8},{1,9},{2,10},{3,11},{4,12},{5,13},{6,14},{7,15},{8,0},{9,1},... | collective-permute-start | bytes 3145736 | tf_op jit(solution)/shard_map/ppermute | solution.py:383
  12.9 65.0 %collective-permute-start.3 = (bf16[256,2048]{1,0:T(8,128)(2,1)S(1)}, bf16[256,2048]{1,0:T(8,128)(2,1)}, u32[]{:S(2)}, u32[]{:S(2)}) collective-permute-start(bf16[256,2048]{1,0:T(8,128)(2,1)S(1)} %shard_map.273.refs_0_.x_ref), channel_id=1, source_target_pairs={{0,4},{1,5},{2,6},{3,7},{4,0},{5,1},{6,2},{7,3},{8,12},{9,13},{10,... | collective-permute-start | bytes 3145736 | tf_op jit(solution)/shard_map/ppermute | solution.py:383
  14.4 63.5 %collective-permute-start = (bf16[256,2048]{1,0:T(8,128)(2,1)}, bf16[256,2048]{1,0:T(8,128)(2,1)S(1)}, u32[]{:S(2)}, u32[]{:S(2)}) collective-permute-start(bf16[256,2048]{1,0:T(8,128)(2,1)} %refs_0_.2), channel_id=1, source_target_pairs={{0,16},{1,17},{2,18},{3,19},{4,20},{5,21},{6,22},{7,23},{8,24},{9,... | collective-permute-start | bytes 3145736 | tf_op jit(solution)/shard_map/ppermute | solution.py:383
  17.4 60.5 %collective-permute-start.1 = (bf16[256,2048]{1,0:T(8,128)(2,1)}, bf16[256,2048]{1,0:T(8,128)(2,1)}, u32[]{:S(2)}, u32[]{:S(2)}) collective-permute-start(bf16[256,2048]{1,0:T(8,128)(2,1)} %refs_0_.2), channel_id=1, source_target_pairs={{0,2},{1,3},{2,0},{3,1},{4,6},{5,7},{6,4},{7,5},{8,10},{9,11},{10,... | collective-permute-start | bytes 3145736 | tf_op jit(solution)/shard_map/ppermute | solution.py:383
  18.9 59.0 %collective-permute-start.4 = (bf16[256,2048]{1,0:T(8,128)(2,1)S(1)}, bf16[256,2048]{1,0:T(8,128)(2,1)}, u32[]{:S(2)}, u32[]{:S(2)}) collective-permute-start(bf16[256,2048]{1,0:T(8,128)(2,1)S(1)} %copy-done.8), channel_id=1, source_target_pairs={{0,4},{1,5},{2,6},{3,7},{4,0},{5,1},{6,2},{7,3},{8,12},{9,13},{10,... | collective-permute-start | bytes 3145736 | tf_op jit(solution)/shard_map/ppermute | solution.py:383
  80.9 54.1 %collective-permute-start.5 = (bf16[8,64,1024]{2,1,0:T(8,128)(2,1)}, bf16[8,64,1024]{2,1,0:T(8,128)(2,1)}, u32[]{:S(2)}, u32[]{:S(2)}) collective-permute-start(bf16[8,64,1024]{2,1,0:T(8,128)(2,1)} %slice.46), channel_id=1, source_target_pairs={{0,16},{1,17},{2,18},{3,19},{4,20},{5,21},{6,22},{7,23},{8,24},{9,... | collective-permute-start | bytes 3145736 | tf_op jit(solution)/shard_map/ppermute | solution.py:383
  83.8 51.3 %collective-permute-start.6 = (bf16[8,64,1024]{2,1,0:T(8,128)(2,1)}, bf16[8,64,1024]{2,1,0:T(8,128)(2,1)}, u32[]{:S(2)}, u32[]{:S(2)}) collective-permute-start(bf16[8,64,1024]{2,1,0:T(8,128)(2,1)} %slice.46), channel_id=1, source_target_pairs={{0,2},{1,3},{2,0},{3,1},{4,6},{5,7},{6,4},{7,5},{8,10},{9,11},{10,... | collective-permute-start | bytes 3145736 | tf_op jit(solution)/shard_map/ppermute | solution.py:383
  85.2 49.8 %collective-permute-start.7 = (bf16[256,2048]{1,0:T(8,128)(2,1)}, bf16[256,2048]{1,0:T(8,128)(2,1)}, u32[]{:S(2)}, u32[]{:S(2)}) collective-permute-start(bf16[256,2048]{1,0:T(8,128)(2,1)} %collective-permute-done.2.refs_1_), channel_id=1, source_target_pairs={{0,4},{1,5},{2,6},{3,7},{4,0},{5,1},{6,2},{7,3},{8,12},{9,13},{10,... | collective-permute-start | bytes 3145736 | tf_op jit(solution)/shard_map/ppermute | solution.py:383
  85.8 49.3 %collective-permute-start.8 = (bf16[256,2048]{1,0:T(8,128)(2,1)S(1)}, bf16[256,2048]{1,0:T(8,128)(2,1)}, u32[]{:S(2)}, u32[]{:S(2)}) collective-permute-start(bf16[256,2048]{1,0:T(8,128)(2,1)S(1)} %copy-done.8), channel_id=1, source_target_pairs={{0,8},{1,9},{2,10},{3,11},{4,12},{5,13},{6,14},{7,15},{8,0},{9,1},... | collective-permute-start | bytes 3145736 | tf_op jit(solution)/shard_map/ppermute | solution.py:383
  87.4 47.6 %collective-permute-start.9 = (bf16[256,2048]{1,0:T(8,128)(2,1)S(1)}, bf16[256,2048]{1,0:T(8,128)(2,1)}, u32[]{:S(2)}, u32[]{:S(2)}) collective-permute-start(bf16[256,2048]{1,0:T(8,128)(2,1)S(1)} %collective-permute-done.refs_2_), channel_id=1, source_target_pairs={{0,2},{1,3},{2,0},{3,1},{4,6},{5,7},{6,4},{7,5},{8,10},{9,11},{10,... | collective-permute-start | bytes 3145736 | tf_op jit(solution)/shard_map/ppermute | solution.py:383
  88.0 47.1 %all-to-all-start.1 = ((bf16[32,16,128]{2,1,0:T(8,128)(2,1)}), bf16[32,16,128]{2,1,0:T(8,128)(2,1)S(1)}, u32[]{:S(2)}, u32[]{:S(2)}) async-start(bf16[32,16,128]{2,1,0:T(8,128)(2,1)} %broadcast_in_dim.14), calls=%async_computation.1 | async-start | bytes 262144 | tf_op jit(solution)/shard_map/all_to_all | solution.py:1142
  167.1 38.7 %collective-permute-start.17 = (bf16[1024,2048]{1,0:T(8,128)(2,1)S(1)}, bf16[1024,2048]{1,0:T(8,128)(2,1)S(1)}, u32[]{:S(2)}, u32[]{:S(2)}) collective-permute-start(bf16[1024,2048]{1,0:T(8,128)(2,1)S(1)} %shard_map.279.refs_0_.ga_ref), channel_id=1, source_target_pairs={{0,1},{1,0},{2,3},{3,2},{4,5},{5,4},{6,7},{7,6},{8,9},{9,8},{10,11... | collective-permute-start | bytes 12582920 | tf_op jit(solution)/shard_map/ppermute | solution.py:383
  167.2 37.7 %collective-permute-start.14 = (bf16[8,64,768]{2,1,0:T(8,128)(2,1)S(1)}, bf16[8,64,768]{2,1,0:T(8,128)(2,1)S(1)}, u32[]{:S(2)}, u32[]{:S(2)}) collective-permute-start(bf16[8,64,768]{2,1,0:T(8,128)(2,1)S(1)} %copy-done.38), channel_id=1, source_target_pairs={{0,16},{1,17},{2,18},{3,19},{4,20},{5,21},{6,22},{7,23},{8,24},{9,... | collective-permute-start | bytes 2359304 | tf_op jit(solution)/shard_map/ppermute | solution.py:383
  168.5 36.4 %collective-permute-start.15 = (bf16[8,64,768]{2,1,0:T(8,128)(2,1)S(1)}, bf16[8,64,768]{2,1,0:T(8,128)(2,1)S(1)}, u32[]{:S(2)}, u32[]{:S(2)}) collective-permute-start(bf16[8,64,768]{2,1,0:T(8,128)(2,1)S(1)} %copy-done.38), channel_id=1, source_target_pairs={{0,2},{1,3},{2,0},{3,1},{4,6},{5,7},{6,4},{7,5},{8,10},{9,11},{10,... | collective-permute-start | bytes 2359304 | tf_op jit(solution)/shard_map/ppermute | solution.py:383
  169.0 32.4 %collective-permute-start.16 = (bf16[64,2048]{1,0:T(8,128)(2,1)S(1)}, bf16[64,2048]{1,0:T(8,128)(2,1)S(1)}, u32[]{:S(2)}, u32[]{:S(2)}) collective-permute-start(bf16[64,2048]{1,0:T(8,128)(2,1)S(1)} %collective-permute-done.11.refs_0_), channel_id=1, source_target_pairs={{0,2},{1,3},{2,0},{3,1},{4,6},{5,7},{6,4},{7,5},{8,10},{9,11},{10,... | collective-permute-start | bytes 786440 | tf_op jit(solution)/shard_map/ppermute | solution.py:383
  227.6 36.3 %collective-permute-start.20 = (bf16[256,2048]{1,0:T(8,128)(2,1)S(1)}, bf16[256,2048]{1,0:T(8,128)(2,1)S(1)}, u32[]{:S(2)}, u32[]{:S(2)}) collective-permute-start(bf16[256,2048]{1,0:T(8,128)(2,1)S(1)} %get-tuple-element.214), channel_id=1, source_target_pairs={{0,2},{1,3},{2,0},{3,1},{4,6},{5,7},{6,4},{7,5},{8,10},{9,11},{10,... | collective-permute-start | bytes 3145736 | tf_op jit(solution)/shard_map/ppermute | solution.py:383
  246.6 39.8 %collective-permute-start.22 = (bf16[256,2048]{1,0:T(8,128)(2,1)S(1)}, bf16[256,2048]{1,0:T(8,128)(2,1)S(1)}, u32[]{:S(2)}, u32[]{:S(2)}) collective-permute-start(bf16[256,2048]{1,0:T(8,128)(2,1)S(1)} %get-tuple-element.234), channel_id=1, source_target_pairs={{0,2},{1,3},{2,0},{3,1},{4,6},{5,7},{6,4},{7,5},{8,10},{9,11},{10,... | collective-permute-start | bytes 3145736 | tf_op jit(solution)/shard_map/ppermute | solution.py:383
  262.6 41.6 %collective-permute-start.23 = (bf16[512,1024]{1,0:T(8,128)(2,1)S(1)}, bf16[512,1024]{1,0:T(8,128)(2,1)S(1)}, u32[]{:S(2)}, u32[]{:S(2)}) collective-permute-start(bf16[512,1024]{1,0:T(8,128)(2,1)S(1)} %get-tuple-element.239), channel_id=1, source_target_pairs={{0,2},{1,3},{2,0},{3,1},{4,6},{5,7},{6,4},{7,5},{8,10},{9,11},{10,... | collective-permute-start | bytes 3145736 | tf_op jit(solution)/shard_map/ppermute | solution.py:383
  264.2 47.1 %collective-permute-start.24 = (bf16[256,2048]{1,0:T(8,128)(2,1)S(1)}, bf16[256,2048]{1,0:T(8,128)(2,1)S(1)}, u32[]{:S(2)}, u32[]{:S(2)}) collective-permute-start(bf16[256,2048]{1,0:T(8,128)(2,1)S(1)} %shard_map.283), channel_id=1, source_target_pairs={{0,16},{1,17},{2,18},{3,19},{4,20},{5,21},{6,22},{7,23},{8,24},{9,... | collective-permute-start | bytes 3145736 | tf_op jit(solution)/shard_map/ppermute | solution.py:383
  311.3 30.8 %collective-permute-start.30 = (bf16[512,1024]{1,0:T(8,128)(2,1)}, bf16[512,1024]{1,0:T(8,128)(2,1)}, u32[]{:S(2)}, u32[]{:S(2)}) collective-permute-start(bf16[512,1024]{1,0:T(8,128)(2,1)} %get-tuple-element.262), channel_id=1, source_target_pairs={{0,2},{1,3},{2,0},{3,1},{4,6},{5,7},{6,4},{7,5},{8,10},{9,11},{10,... | collective-permute-start | bytes 3145736 | tf_op jit(solution)/shard_map/ppermute | solution.py:383
  319.6 55.0 %collective-permute-start.32 = (bf16[512,1024]{1,0:T(8,128)(2,1)}, bf16[512,1024]{1,0:T(8,128)(2,1)}, u32[]{:S(2)}, u32[]{:S(2)}) collective-permute-start(bf16[512,1024]{1,0:T(8,128)(2,1)} %shard_map.287), channel_id=1, source_target_pairs={{0,16},{1,17},{2,18},{3,19},{4,20},{5,21},{6,22},{7,23},{8,24},{9,... | collective-permute-start | bytes 3145736 | tf_op jit(solution)/shard_map/ppermute | solution.py:383
  334.0 40.6 %collective-permute-start.31 = (bf16[512,768]{1,0:T(8,128)(2,1)}, bf16[512,768]{1,0:T(8,128)(2,1)S(1)}, u32[]{:S(2)}, u32[]{:S(2)}) collective-permute-start(bf16[512,768]{1,0:T(8,128)(2,1)} %get-tuple-element.275), channel_id=1, source_target_pairs={{0,2},{1,3},{2,0},{3,1},{4,6},{5,7},{6,4},{7,5},{8,10},{9,11},{10,... | collective-permute-start | bytes 2359304 | tf_op jit(solution)/shard_map/ppermute | solution.py:383
  335.5 39.2 %collective-permute-start.33 = (bf16[256,2048]{1,0:T(8,128)(2,1)}, bf16[256,2048]{1,0:T(8,128)(2,1)S(1)}, u32[]{:S(2)}, u32[]{:S(2)}) collective-permute-start(bf16[256,2048]{1,0:T(8,128)(2,1)} %copy-done.42), channel_id=1, source_target_pairs={{0,4},{1,5},{2,6},{3,7},{4,0},{5,1},{6,2},{7,3},{8,12},{9,13},{10,... | collective-permute-start | bytes 3145736 | tf_op jit(solution)/shard_map/ppermute | solution.py:383
  347.4 42.3 %collective-permute-start.40 = (bf16[256,2048]{1,0:T(8,128)(2,1)}, bf16[256,2048]{1,0:T(8,128)(2,1)}, u32[]{:S(2)}, u32[]{:S(2)}) collective-permute-start(bf16[256,2048]{1,0:T(8,128)(2,1)} %shard_map.291), channel_id=1, source_target_pairs={{0,8},{1,9},{2,10},{3,11},{4,12},{5,13},{6,14},{7,15},{8,0},{9,1},... | collective-permute-start | bytes 3145736 | tf_op jit(solution)/shard_map/ppermute | solution.py:383
  379.1 27.7 %all-to-all-start.2 = ((bf16[8,64,1024]{2,1,0:T(8,128)(2,1)}), bf16[8,64,1024]{2,1,0:T(8,128)(2,1)S(1)}, u32[]{:S(2)}, u32[]{:S(2)}) async-start(bf16[8,64,1024]{2,1,0:T(8,128)(2,1)} %bitcast.42), calls=%async_computation.2 | async-start | bytes 2097152 | tf_op jit(solution)/shard_map/all_to_all | solution.py:185
  389.7 40.7 %collective-permute-start.34 = (bf16[512,768]{1,0:T(8,128)(2,1)}, bf16[512,768]{1,0:T(8,128)(2,1)}, u32[]{:S(2)}, u32[]{:S(2)}) collective-permute-start(bf16[512,768]{1,0:T(8,128)(2,1)} %copy-done.40), channel_id=1, source_target_pairs={{0,16},{1,17},{2,18},{3,19},{4,20},{5,21},{6,22},{7,23},{8,24},{9,... | collective-permute-start | bytes 2359304 | tf_op jit(solution)/shard_map/ppermute | solution.py:383
  389.7 40.7 %collective-permute-start.35 = (bf16[512,768]{1,0:T(8,128)(2,1)}, bf16[512,768]{1,0:T(8,128)(2,1)}, u32[]{:S(2)}, u32[]{:S(2)}) collective-permute-start(bf16[512,768]{1,0:T(8,128)(2,1)} %copy-done.43), channel_id=1, source_target_pairs={{0,2},{1,3},{2,0},{3,1},{4,6},{5,7},{6,4},{7,5},{8,10},{9,11},{10,... | collective-permute-start | bytes 2359304 | tf_op jit(solution)/shard_map/ppermute | solution.py:383
  391.3 39.2 %collective-permute-start.41 = (bf16[128,2048]{1,0:T(8,128)(2,1)}, bf16[128,2048]{1,0:T(8,128)(2,1)}, u32[]{:S(2)}, u32[]{:S(2)}) collective-permute-start(bf16[128,2048]{1,0:T(8,128)(2,1)} %copy-done.53), channel_id=1, source_target_pairs={{0,2},{1,3},{2,0},{3,1},{4,6},{5,7},{6,4},{7,5},{8,10},{9,11},{10,... | collective-permute-start | bytes 1572872 | tf_op jit(solution)/shard_map/ppermute | solution.py:383
  410.5 28.7 %collective-permute-start.43 = (bf16[256,2048]{1,0:T(8,128)(2,1)}, bf16[256,2048]{1,0:T(8,128)(2,1)}, u32[]{:S(2)}, u32[]{:S(2)}) collective-permute-start(bf16[256,2048]{1,0:T(8,128)(2,1)} %copy-done.41), channel_id=1, source_target_pairs={{0,4},{1,5},{2,6},{3,7},{4,0},{5,1},{6,2},{7,3},{8,12},{9,13},{10,... | collective-permute-start | bytes 3145736 | tf_op jit(solution)/shard_map/ppermute | solution.py:383
  444.7 33.8 %collective-permute-start.45 = (bf16[256,2048]{1,0:T(8,128)(2,1)}, bf16[256,2048]{1,0:T(8,128)(2,1)}, u32[]{:S(2)}, u32[]{:S(2)}) collective-permute-start(bf16[256,2048]{1,0:T(8,128)(2,1)} %shard_map.295), channel_id=1, source_target_pairs={{0,8},{1,9},{2,10},{3,11},{4,12},{5,13},{6,14},{7,15},{8,0},{9,1},... | collective-permute-start | bytes 3145736 | tf_op jit(solution)/shard_map/ppermute | solution.py:383
  446.6 31.9 %collective-permute-start.46 = (bf16[256,2048]{1,0:T(8,128)(2,1)}, bf16[256,2048]{1,0:T(8,128)(2,1)}, u32[]{:S(2)}, u32[]{:S(2)}) collective-permute-start(bf16[256,2048]{1,0:T(8,128)(2,1)} %get-tuple-element.325), channel_id=1, source_target_pairs={{0,4},{1,5},{2,6},{3,7},{4,0},{5,1},{6,2},{7,3},{8,12},{9,13},{10,... | collective-permute-start | bytes 3145736 | tf_op jit(solution)/shard_map/ppermute | solution.py:383
  (104 other events, 980.5 us)
where the time goes:
time: 496 us; the launch traced here: 487 us
  Pallas kernels  190 us (38%)
  waiting for transfers between devices  163 us (33%)
  starting transfers between devices  64.9 us (13%)
  local copies, waits for them, and re-layouts  57.2 us (12%)
  other arithmetic  9.69 us (2%)
    pallas_call x17, Pallas kernels, call(): pl.pallas_call(body, grid=grid, in_specs=in_specs, out_specs=out_specs, *...  114 us
    ppermute x45, waiting for transfers between devices, flip(): lax.ppermute(value, AXIS, [(d, d ^ 1 << bit) for d in range(lax.axis_size...  98.5 us
    pallas_call x8, Pallas kernels, call(): return pl.pallas_call(body, grid_spec=spec, **extra)(scalars, *args)  51 us
    unnamed x170, local copies, waits for them, and re-layouts  48.4 us
    ppermute x45, starting transfers between devices, flip(): lax.ppermute(value, AXIS, [(d, d ^ 1 << bit) for d in range(lax.axis_size...  42 us
    all_to_all x1, waiting for transfers between devices, local_tuned(): small = lax.all_to_all(small, AXIS, split_axis=0, concat_axis=0, tiled=True)  41.5 us
    all_to_all x1, waiting for transfers between devices, local_tuned(): sums = lax.all_to_all(flat, AXIS, split_axis=0, concat_axis=0, tiled=True)  18.1 us
    pallas_call x1, Pallas kernels, norms(): pl.pallas_call(body, grid=(1,), in_specs=[pl.BlockSpec((8, width), lambda...  13.6 us
  transfers between devices with their start and end apart: 52, of which 11 were waited for; matrix products, arithmetic and copies ran while one was open for 3% of the time, Pallas kernels for 38%

commit v1 on v0

--- a/solution.py
+++ b/solution.py
@@ -133,8 +133,9 @@
     def flip(self, value, bit):
         return lax.ppermute(value, AXIS, [(d, d ^ (1 << bit)) for d in range(self.count)])
 
-    def exchange_heads(self, value):
-        return lax.ppermute(value, AXIS, [(d, self.swapped(d)) for d in range(self.count)])
+    def exchange_heads(self, value, flipped=0, back=False):
+        pairs = [(d, self.swapped(d ^ flipped)) for d in range(self.count)]
+        return lax.ppermute(value, AXIS, [(b, a) for a, b in pairs] if back else pairs)
 
     def mine(self, bit):
         return (lax.axis_index(AXIS) >> bit) & 1
@@ -1167,16 +1168,16 @@
     xb = flip(xa, CORE)
     up_xz = flip(up_z, X)
     g3 = flip(g1, Y)
+    proj_z = lay.exchange_heads(proj0, 1 << ZH, back=True)
     proj0 = lay.exchange_heads(proj0)
     w_down = join_units([down_weight, down_x, down_z, down_xz], mine)
-    gains, g0, g1, g2, g3, qkv_cols, proj0, up_xz, xb, w_down = after(
-        (gains, g0, g1, g2, g3, qkv_cols, proj0, up_xz, xb, w_down)
+    gains, g0, g1, g2, g3, qkv_cols, proj0, proj_z, up_xz, xb, w_down = after(
+        (gains, g0, g1, g2, g3, qkv_cols, proj0, proj_z, up_xz, xb, w_down)
     )
     ga = join([g0, g1, g2, g3])
     gb = flip(ga, CORE)
     qkv_z = flip(qkv_cols, ZH)
     qkv_x = flip(qkv_cols, X)
-    proj_z = flip(proj0, ZH)
     proj_x = flip(proj0, X)
     first, second, stats = norms([xa, xb], gains, count)
     w_up = [v.reshape(-1, hidden) for v in (up_cols, up_z, up_x, up_xz)]
@@ -1261,9 +1262,10 @@
     qkv_sum = (qkv_k0 + qkv_g0.astype(F32) + qkv_got.astype(F32)).astype(BF16)
     qkv_back = lay.to_columns(qkv_sum.reshape(8, rows, 3 * HEAD))
     proj_sum = (proj_k + proj_g.astype(F32)).reshape(2, rows, width)
-    proj_kept = lax.dynamic_index_in_dim(proj_sum, mzh, 0, keepdims=False)
+    proj_kept = lax.dynamic_index_in_dim(proj_sum, mzh, 0, keepdims=False).astype(BF16)
     proj_sent = lax.dynamic_index_in_dim(proj_sum, 1 - mzh, 0, keepdims=False).astype(BF16)
-    proj_got = flip(proj_sent, ZH)
+    proj_own = lay.exchange_heads(proj_kept)
+    proj_got = lay.exchange_heads(proj_sent, 1 << ZH)
     edge_g1, edge_s0, qkv_sum, proj_sent = after((edge_g1, edge_s0, qkv_sum, proj_sent))
     edge_g0 = flip(edge_s0, Y)
     edge_sent = add_half(edge_k, edge_g1, count, 1)
@@ -1273,12 +1275,12 @@
     grad_qkv = join_qkv(qkv_back)
     layer_out = total([inputs, b_out, out_k, out_g0, out_got], count)
     grad_down = total([down_k0, down_g0, down_got], unit)
-    proj_got, edge_k, layer_out, grad_down = after((proj_got, edge_k, layer_out, grad_down))
-    proj_back = lay.exchange_heads((proj_kept + proj_got.astype(F32)).astype(BF16))
-    edge_got, edge_g0, edge_k = after((edge_got, edge_g0, edge_k))
+    edge_got, edge_g0, edge_k, layer_out, grad_down, grad_up, grad_qkv = after(
+        (edge_got, edge_g0, edge_k, layer_out, grad_down, grad_up, grad_qkv)
+    )
     grad_inputs = finish(edge_k, edge_g0, edge_got, x0, cotangent, mine)
-    proj_back, grad_inputs = after((proj_back, grad_inputs))
-    grad_proj = proj_back.astype(F32)
+    proj_own, proj_got, grad_inputs = after((proj_own, proj_got, grad_inputs))
+    grad_proj = proj_own.astype(F32) + proj_got.astype(F32)
     sums = jnp.sum(sums, axis=0)
     got, at = [], 0
     for size in [rows] * 5 + [3 * rows, unit]:

time: 496 us -> 489 us (0.986)
  waiting for transfers between devices: 163 us -> 155 us
    ppermute x45 -> x43, waiting for transfers between devices: 98.5 us -> 91.6 us  [flip(): lax.ppermute(value, AXIS, [(d, d ^ 1 << bit) for d in range(lax.axis_size...]
    ppermute x2 -> x4, starting transfers between devices: 2.91 us -> 8.52 us  [exchange_heads(): lax.ppermute(value, AXIS, [(b, a) for a, b in pairs] if back else pairs)]
    ppermute x45 -> x43, starting transfers between devices: 42 us -> 39.2 us  [flip(): lax.ppermute(value, AXIS, [(d, d ^ 1 << bit) for d in range(lax.axis_size...]
    unnamed x170 -> x166, local copies, waits for them, and re-layouts: 48.4 us -> 48 us
where the time goes in v1:
time: 489 us; the launch traced here: 484 us
  Pallas kernels  192 us (39%)
  waiting for transfers between devices  155 us (32%)
  starting transfers between devices  67.8 us (14%)
  local copies, waits for them, and re-layouts  57.5 us (12%)
  other arithmetic  9.7 us (2%)
    pallas_call x17, Pallas kernels, call(): pl.pallas_call(body, grid=grid, in_specs=in_specs, out_specs=out_specs, *...  114 us
    ppermute x43, waiting for transfers between devices, flip(): lax.ppermute(value, AXIS, [(d, d ^ 1 << bit) for d in range(lax.axis_size...  91.6 us
    pallas_call x8, Pallas kernels, call(): return pl.pallas_call(body, grid_spec=spec, **extra)(scalars, *args)  52.4 us
    unnamed x166, local copies, waits for them, and re-layouts  48 us
    all_to_all x1, waiting for transfers between devices, local_tuned(): small = lax.all_to_all(small, AXIS, split_axis=0, concat_axis=0, tiled=True)  41.5 us
    ppermute x43, starting transfers between devices, flip(): lax.ppermute(value, AXIS, [(d, d ^ 1 << bit) for d in range(lax.axis_size...  39.2 us
    all_to_all x1, waiting for transfers between devices, local_tuned(): sums = lax.all_to_all(flat, AXIS, split_axis=0, concat_axis=0, tiled=True)  17.8 us
    pallas_call x1, Pallas kernels, norms(): pl.pallas_call(body, grid=(1,), in_specs=[pl.BlockSpec((8, width), lambda...  13.6 us
  transfers between devices with their start and end apart: 52, of which 11 were waited for; matrix products, arithmetic and copies ran while one was open for 3% of the time, Pallas kernels for 38%

profile of v1, /device:TPU:0, one launch (start us, length us, event | category | flops | bytes accessed | tf_op | source)
XLA Modules:
  0.0 484.1 jit_solution(8042166058841116290)
XLA Ops:
  4.5 5.4 %all-to-all-start = ((bf16[8,64,1792]{2,1,0:T(8,128)(2,1)}), bf16[8,64,1792]{2,1,0:T(8,128)(2,1)}, u32[]{:S(2)}, u32[]{:S(2)}) async-start(bf16[8,64,1792]{2,1,0:T(8,128)(2,1)} %copy-done.9), calls=%async_computation | async-start | bytes 3670016 | tf_op jit(solution)/shard_map/all_to_all | solution.py:186
  19.6 58.3 %collective-permute-done.2.refs_1_ = bf16[256,2048]{1,0:T(8,128)(2,1)} collective-permute-done((bf16[256,2048]{1,0:T(8,128)(2,1)S(1)}, bf16[256,2048]{1,0:T(8,128)(2,1)}, u32[]{:S(2)}, u32[]{:S(2)}) %collective-permute-start.2) | collective-permute-done | bytes 1048608 | tf_op jit(solution)/shard_map/ppermute | solution.py:384
  88.0 3.5 all-to-all-start.1
  93.6 41.5 %all-to-all-done.1.small_ref = bf16[32,16,128]{2,1,0:T(8,128)(2,1)S(1)} async-done(((bf16[32,16,128]{2,1,0:T(8,128)(2,1)}), bf16[32,16,128]{2,1,0:T(8,128)(2,1)S(1)}, u32[]{:S(2)}, u32[]{:S(2)}) %all-to-all-start.1) | async-done | bytes 131104 | tf_op jit(solution)/shard_map/all_to_all | solution.py:1143
  135.1 3.5 shard_map.275.a_ref.xa_ref
  141.8 3.3 collective-permute-start.12
  146.5 6.0 %shard_map.274 = (f32[8,2048]{1,0:T(8,128)S(1)}, f32[1,2048]{1,0:T(1,128)S(1)}, f32[1,1024]{1,0:T(1,128)S(1)}, f32[1,768]{1,0:T(1,128)S(1)}, f32[8,1,256]{2,1,0:...) custom-call(s32[6]{0:T(128)S(1)} %stack.32.place_ref, bf16[32,16,128]{2,1,0:T(8,128)(2,1)S(1)} %all-to-all-done.1.small_ref, ...), custom_call_target="tpu_custom_call" | custom-call | flops 450000000 | bytes 1024 | tf_op jit(solution)/shard_map/pallas_call | solution.py:554
  161.3 3.3 collective-permute-done.10.refs_3_
  170.6 13.6 %shard_map.277 = (bf16[2048,2048]{1,0:T(8,128)(2,1)}, bf16[2048,2048]{1,0:T(8,128)(2,1)}, f32[2048,128]{1,0:T(8,128)S(1)}) custom-call(f32[8,2048]{1,0:T(8,128)S(1)} %get-tuple-element.196.v_ref, bf16[1024,2048]{1,0:T(8,128)(2,1)} %shard_map.275.a_ref.xa_ref, bf16[1024,2048]{1,0:T(8,128)(2,1)} %collective-permute-done.14.b_ref.xb_ref), custom_call_target="tpu_custom_call" | custom-call | flops 5400000000 | bytes 1024 | tf_op jit(solution)/shard_map/pallas_call | solution.py:679
  185.2 16.2 %shard_map.278 = (bf16[2048,1024]{1,0:T(8,128)(2,1)S(1)}, f32[2048,1024]{1,0:T(8,128)}) custom-call(bf16[2048,2048]{1,0:T(8,128)(2,1)} %get-tuple-element.198.s_ref.l_ref, bf16[512,1024]{1,0:T(8,128)(2,1)} %bitcast.7.refs_0_, bf16[512,1024]{1,0:T(8,128)(2,1)} %bitcast.8.refs_1_, bf16[512,1024]{1,0:T(8,128)(2,1)} %bitcast.9.refs_2_, ...), custom_call_target="tpu_custom_call" | custom-call | flops 7200000000 | bytes 1024 | tf_op jit(solution)/shard_map/pallas_call | solution.py:395
  201.4 3.5 collective-permute-done.15
  208.9 14.7 %shard_map.280 = (bf16[256,2048]{1,0:T(8,128)(2,1)S(1)}, bf16[256,2048]{1,0:T(8,128)(2,1)S(1)}, f32[256,2048]{1,0:T(8,128)S(1)}, f32[256,2048]{1,0:T(8,128)S(1)}) custom-call(s32[2]{0:T(128)S(1)} %pad_add_fusion.mine_ref, bf16[2048,1024]{1,0:T(8,128)(2,1)S(1)} %get-tuple-element.240.l_ref.a_ref, bf16[1024,2048]{1,0:T(8,128)(2,1)} %copy-done, ...), custom_call_target="tpu_custom_call" | custom-call | flops 6750000128 | bytes 1024 | tf_op jit(solution)/shard_map/pallas_call | solution.py:397
  231.3 12.5 %shard_map.281 = (bf16[2048,1024]{1,0:T(8,128)(2,1)S(1)}, f32[1,1024]{1,0:T(1,128)S(1)}) custom-call(bf16[1024,2048]{1,0:T(8,128)(2,1)S(1)} %copy-done.1, bf16[1024,2048]{1,0:T(8,128)(2,1)S(1)} %copy-done.11, bf16[1024,2048]{1,0:T(8,128)(2,1)} %copy-done.13, f32[2048,1024]{1,0:T(8,128)} %get-tuple-element.219.slope_ref), custom_call_target="tpu_custom_call" | custom-call | flops 6300000256 | bytes 1024 | tf_op jit(solution)/shard_map/pallas_call | solution.py:395
  250.1 13.0 %shard_map.282 = (bf16[512,1024]{1,0:T(8,128)(2,1)S(1)}, bf16[512,1024]{1,0:T(8,128)(2,1)}, f32[512,1024]{1,0:T(8,128)S(1)}, f32[512,1024]{1,0:T(8,128)S(1)}) custom-call(s32[2]{0:T(128)S(1)} %pad_add_fusion.mine_ref, bf16[2048,2048]{1,0:T(8,128)(2,1)} %get-tuple-element.198.s_ref.l_ref, bf16[2048,1024]{1,0:T(8,128)(2,1)S(1)} %copy-done.57), custom_call_target="tpu_custom_call" | custom-call | flops 5400000000 | bytes 1024 | tf_op jit(solution)/shard_map/pallas_call | solution.py:397
  266.8 17.7 %shard_map.285 = (bf16[2048,256]{1,0:T(8,128)(2,1)S(1)}, bf16[2048,768]{1,0:T(8,128)(2,1)S(1)}, f32[1,768]{1,0:T(1,128)S(1)}) custom-call(bf16[2048,2048]{1,0:T(8,128)(2,1)} %get-tuple-element.226.f_ref.l_ref, bf16[512,768]{1,0:T(8,128)(2,1)S(1)} %bitcast.32, bf16[512,768]{1,0:T(8,128)(2,1)S(1)} %bitcast.34, bf16[512,768]{1,0:T(8,128)(2,1)S(1)} %bitcast.36, ...), custom_call_target="tpu_custom_call" | custom-call | flops 7649999872 | bytes 1024 | tf_op jit(solution)/shard_map/pallas_call | solution.py:395
  286.3 15.2 %shard_map.286 = (bf16[256,2048]{1,0:T(8,128)(2,1)S(1)}, bf16[256,2048]{1,0:T(8,128)(2,1)S(1)}, bf16[256,2048]{1,0:T(8,128)(2,1)S(1)}, bf16[256,2048]{1,0:T(8,128)(2,1)S(1)}, bf16[1024,2048]{1,0:T(8,128)(2,1)S(1)}) custom-call(bf16[2048,1024]{1,0:T(8,128)(2,1)} %copy-done.66, bf16[1024,2048]{1,0:T(8,128)(2,1)} %copy-done.13, ...), custom_call_target="tpu_custom_call" | custom-call | flops 7200000000 | bytes 1024 | tf_op jit(solution)/shard_map/pallas_call | solution.py:395
  304.6 7.0 %collective-permute-done.24.refs_2_ = bf16[256,2048]{1,0:T(8,128)(2,1)S(1)} collective-permute-done((bf16[256,2048]{1,0:T(8,128)(2,1)S(1)}, bf16[256,2048]{1,0:T(8,128)(2,1)S(1)}, u32[]{:S(2)}, u32[]{:S(2)}) %collective-permute-start.24) | collective-permute-done | bytes 1048608 | tf_op jit(solution)/shard_map/ppermute | solution.py:384
  313.3 4.3 shard_map.288
  321.9 11.1 %shard_map.289 = (bf16[512,768]{1,0:T(8,128)(2,1)}, bf16[512,768]{1,0:T(8,128)(2,1)S(1)}, f32[512,768]{1,0:T(8,128)S(1)}, f32[512,768]{1,0:T(8,128)S(1)}) custom-call(s32[2]{0:T(128)S(1)} %pad_add_fusion.mine_ref, bf16[2048,2048]{1,0:T(8,128)(2,1)} %get-tuple-element.226.f_ref.l_ref, bf16[2048,768]{1,0:T(8,128)(2,1)S(1)} %copy-done.63), custom_call_target="tpu_custom_call" | custom-call | flops 4499999744 | bytes 1024 | tf_op jit(solution)/shard_map/pallas_call | solution.py:397
  337.9 3.8 shard_map.290
  341.8 3.2 collective-permute-done.29.g_ref
  347.6 27.1 %shard_map.292 = (bf16[256,2048]{1,0:T(8,128)(2,1)}, bf16[256,2048]{1,0:T(8,128)(2,1)}, bf16[256,2048]{1,0:T(8,128)(2,1)}, bf16[256,2048]{1,0:T(8,128)(2,1)}, bf...) custom-call(bf16[2048,1024]{1,0:T(8,128)(2,1)} %copy-done.56, bf16[2048,768]{1,0:T(8,128)(2,1)} %copy-done.62, ...), custom_call_target="tpu_custom_call" | custom-call | flops 12600000512 | bytes 1024 | tf_op jit(solution)/shard_map/pallas_call | solution.py:395
  379.2 3.6 all-to-all-start.2
  383.0 6.7 %collective-permute-done.40.refs_4_ = bf16[256,2048]{1,0:T(8,128)(2,1)} collective-permute-done((bf16[256,2048]{1,0:T(8,128)(2,1)}, bf16[256,2048]{1,0:T(8,128)(2,1)}, u32[]{:S(2)}, u32[]{:S(2)}) %collective-permute-start.40) | collective-permute-done | bytes 1048608 | tf_op jit(solution)/shard_map/ppermute | solution.py:384
  392.0 5.6 %shard_map.294 = (bf16[256,2048]{1,0:T(8,128)(2,1)S(1)}, bf16[256,2048]{1,0:T(8,128)(2,1)}, f32[512,2048]{1,0:T(8,128)S(1)}) custom-call(bf16[1024,2048]{1,0:T(8,128)(2,1)} %get-tuple-element.293.k_ref, bf16[256,2048]{1,0:T(8,128)(2,1)} %collective-permute-done.36.refs_0_, bf16[256,2048]{1,0:T(8,128)(2,1)} %collective-permute-done.37.refs_1_, ...), custom_call_target="tpu_custom_call" | custom-call | flops 2249999872 | bytes 1024 | tf_op jit(solution)/shard_map/pallas_call | solution.py:395
  401.7 4.4 all-to-all-done.2.p_ref
  406.9 3.3 all-to-all-start.3
  412.0 17.8 %all-to-all-done.3 = f32[32,1,768]{2,1,0:T(1,128)S(1)} async-done(((f32[32,1,768]{2,1,0:T(1,128)}), f32[32,1,768]{2,1,0:T(1,128)S(1)}, u32[]{:S(2)}, u32[]{:S(2)}) %all-to-all-start.3) | async-done | bytes 98336 | tf_op jit(solution)/shard_map/all_to_all | solution.py:1260
  432.8 4.2 all-to-all-start.4
  448.5 3.6 collective-permute-start.45
  467.7 9.1 %collective-permute-done.43.b_ref = bf16[256,2048]{1,0:T(8,128)(2,1)} collective-permute-done((bf16[256,2048]{1,0:T(8,128)(2,1)}, bf16[256,2048]{1,0:T(8,128)(2,1)}, u32[]{:S(2)}, u32[]{:S(2)}) %collective-permute-start.43) | collective-permute-done | bytes 1048608 | tf_op jit(solution)/shard_map/ppermute | solution.py:384
  476.8 4.6 shard_map.300
  (309 shorter events, 131.5 us)
Async XLA Ops:
  4.5 73.4 %all-to-all-start = ((bf16[8,64,1792]{2,1,0:T(8,128)(2,1)}), bf16[8,64,1792]{2,1,0:T(8,128)(2,1)}, u32[]{:S(2)}, u32[]{:S(2)}) async-start(bf16[8,64,1792]{2,1,0:T(8,128)(2,1)} %copy-done.9), calls=%async_computation | async-start | bytes 3670016 | tf_op jit(solution)/shard_map/all_to_all | solution.py:186
  10.8 67.1 %collective-permute-start.2 = (bf16[256,2048]{1,0:T(8,128)(2,1)S(1)}, bf16[256,2048]{1,0:T(8,128)(2,1)}, u32[]{:S(2)}, u32[]{:S(2)}) collective-permute-start(bf16[256,2048]{1,0:T(8,128)(2,1)S(1)} %shard_map.273.refs_0_.x_ref), channel_id=1, source_target_pairs={{0,8},{1,9},{2,10},{3,11},{4,12},{5,13},{6,14},{7,15},{8,0},{9,1},... | collective-permute-start | bytes 3145736 | tf_op jit(solution)/shard_map/ppermute | solution.py:384
  12.9 65.0 %collective-permute-start.3 = (bf16[256,2048]{1,0:T(8,128)(2,1)S(1)}, bf16[256,2048]{1,0:T(8,128)(2,1)}, u32[]{:S(2)}, u32[]{:S(2)}) collective-permute-start(bf16[256,2048]{1,0:T(8,128)(2,1)S(1)} %shard_map.273.refs_0_.x_ref), channel_id=1, source_target_pairs={{0,4},{1,5},{2,6},{3,7},{4,0},{5,1},{6,2},{7,3},{8,12},{9,13},{10,... | collective-permute-start | bytes 3145736 | tf_op jit(solution)/shard_map/ppermute | solution.py:384
  14.4 63.4 %collective-permute-start = (bf16[256,2048]{1,0:T(8,128)(2,1)}, bf16[256,2048]{1,0:T(8,128)(2,1)S(1)}, u32[]{:S(2)}, u32[]{:S(2)}) collective-permute-start(bf16[256,2048]{1,0:T(8,128)(2,1)} %refs_0_.2), channel_id=1, source_target_pairs={{0,16},{1,17},{2,18},{3,19},{4,20},{5,21},{6,22},{7,23},{8,24},{9,... | collective-permute-start | bytes 3145736 | tf_op jit(solution)/shard_map/ppermute | solution.py:384
  17.4 60.5 %collective-permute-start.1 = (bf16[256,2048]{1,0:T(8,128)(2,1)}, bf16[256,2048]{1,0:T(8,128)(2,1)}, u32[]{:S(2)}, u32[]{:S(2)}) collective-permute-start(bf16[256,2048]{1,0:T(8,128)(2,1)} %refs_0_.2), channel_id=1, source_target_pairs={{0,2},{1,3},{2,0},{3,1},{4,6},{5,7},{6,4},{7,5},{8,10},{9,11},{10,... | collective-permute-start | bytes 3145736 | tf_op jit(solution)/shard_map/ppermute | solution.py:384
  18.9 59.0 %collective-permute-start.4 = (bf16[256,2048]{1,0:T(8,128)(2,1)S(1)}, bf16[256,2048]{1,0:T(8,128)(2,1)}, u32[]{:S(2)}, u32[]{:S(2)}) collective-permute-start(bf16[256,2048]{1,0:T(8,128)(2,1)S(1)} %copy-done.8), channel_id=1, source_target_pairs={{0,4},{1,5},{2,6},{3,7},{4,0},{5,1},{6,2},{7,3},{8,12},{9,13},{10,... | collective-permute-start | bytes 3145736 | tf_op jit(solution)/shard_map/ppermute | solution.py:384
  80.9 54.1 %collective-permute-start.5 = (bf16[8,64,1024]{2,1,0:T(8,128)(2,1)}, bf16[8,64,1024]{2,1,0:T(8,128)(2,1)}, u32[]{:S(2)}, u32[]{:S(2)}) collective-permute-start(bf16[8,64,1024]{2,1,0:T(8,128)(2,1)} %slice.46), channel_id=1, source_target_pairs={{0,16},{1,17},{2,18},{3,19},{4,20},{5,21},{6,22},{7,23},{8,24},{9,... | collective-permute-start | bytes 3145736 | tf_op jit(solution)/shard_map/ppermute | solution.py:384
  83.8 51.3 %collective-permute-start.6 = (bf16[8,64,1024]{2,1,0:T(8,128)(2,1)}, bf16[8,64,1024]{2,1,0:T(8,128)(2,1)}, u32[]{:S(2)}, u32[]{:S(2)}) collective-permute-start(bf16[8,64,1024]{2,1,0:T(8,128)(2,1)} %slice.46), channel_id=1, source_target_pairs={{0,2},{1,3},{2,0},{3,1},{4,6},{5,7},{6,4},{7,5},{8,10},{9,11},{10,... | collective-permute-start | bytes 3145736 | tf_op jit(solution)/shard_map/ppermute | solution.py:384
  85.3 49.8 %collective-permute-start.7 = (bf16[256,2048]{1,0:T(8,128)(2,1)}, bf16[256,2048]{1,0:T(8,128)(2,1)}, u32[]{:S(2)}, u32[]{:S(2)}) collective-permute-start(bf16[256,2048]{1,0:T(8,128)(2,1)} %collective-permute-done.2.refs_1_), channel_id=1, source_target_pairs={{0,4},{1,5},{2,6},{3,7},{4,0},{5,1},{6,2},{7,3},{8,12},{9,13},{10,... | collective-permute-start | bytes 3145736 | tf_op jit(solution)/shard_map/ppermute | solution.py:384
  85.8 49.3 %collective-permute-start.8 = (bf16[256,2048]{1,0:T(8,128)(2,1)S(1)}, bf16[256,2048]{1,0:T(8,128)(2,1)}, u32[]{:S(2)}, u32[]{:S(2)}) collective-permute-start(bf16[256,2048]{1,0:T(8,128)(2,1)S(1)} %copy-done.8), channel_id=1, source_target_pairs={{0,8},{1,9},{2,10},{3,11},{4,12},{5,13},{6,14},{7,15},{8,0},{9,1},... | collective-permute-start | bytes 3145736 | tf_op jit(solution)/shard_map/ppermute | solution.py:384
  87.4 47.6 %collective-permute-start.9 = (bf16[256,2048]{1,0:T(8,128)(2,1)S(1)}, bf16[256,2048]{1,0:T(8,128)(2,1)}, u32[]{:S(2)}, u32[]{:S(2)}) collective-permute-start(bf16[256,2048]{1,0:T(8,128)(2,1)S(1)} %collective-permute-done.refs_2_), channel_id=1, source_target_pairs={{0,2},{1,3},{2,0},{3,1},{4,6},{5,7},{6,4},{7,5},{8,10},{9,11},{10,... | collective-permute-start | bytes 3145736 | tf_op jit(solution)/shard_map/ppermute | solution.py:384
  88.0 47.1 %all-to-all-start.1 = ((bf16[32,16,128]{2,1,0:T(8,128)(2,1)}), bf16[32,16,128]{2,1,0:T(8,128)(2,1)S(1)}, u32[]{:S(2)}, u32[]{:S(2)}) async-start(bf16[32,16,128]{2,1,0:T(8,128)(2,1)} %broadcast_in_dim.14), calls=%async_computation.1 | async-start | bytes 262144 | tf_op jit(solution)/shard_map/all_to_all | solution.py:1143
  167.1 38.7 %collective-permute-start.18 = (bf16[1024,2048]{1,0:T(8,128)(2,1)S(1)}, bf16[1024,2048]{1,0:T(8,128)(2,1)S(1)}, u32[]{:S(2)}, u32[]{:S(2)}) collective-permute-start(bf16[1024,2048]{1,0:T(8,128)(2,1)S(1)} %shard_map.279.refs_0_.ga_ref), channel_id=1, source_target_pairs={{0,1},{1,0},{2,3},{3,2},{4,5},{5,4},{6,7},{7,6},{8,9},{9,8},{10,11... | collective-permute-start | bytes 12582920 | tf_op jit(solution)/shard_map/ppermute | solution.py:384
  167.2 37.7 %collective-permute-start.15 = (bf16[8,64,768]{2,1,0:T(8,128)(2,1)S(1)}, bf16[8,64,768]{2,1,0:T(8,128)(2,1)S(1)}, u32[]{:S(2)}, u32[]{:S(2)}) collective-permute-start(bf16[8,64,768]{2,1,0:T(8,128)(2,1)S(1)} %copy-done.38), channel_id=1, source_target_pairs={{0,16},{1,17},{2,18},{3,19},{4,20},{5,21},{6,22},{7,23},{8,24},{9,... | collective-permute-start | bytes 2359304 | tf_op jit(solution)/shard_map/ppermute | solution.py:384
  168.5 36.4 %collective-permute-start.16 = (bf16[8,64,768]{2,1,0:T(8,128)(2,1)S(1)}, bf16[8,64,768]{2,1,0:T(8,128)(2,1)S(1)}, u32[]{:S(2)}, u32[]{:S(2)}) collective-permute-start(bf16[8,64,768]{2,1,0:T(8,128)(2,1)S(1)} %copy-done.38), channel_id=1, source_target_pairs={{0,2},{1,3},{2,0},{3,1},{4,6},{5,7},{6,4},{7,5},{8,10},{9,11},{10,... | collective-permute-start | bytes 2359304 | tf_op jit(solution)/shard_map/ppermute | solution.py:384
  169.0 32.4 %collective-permute-start.17 = (bf16[64,2048]{1,0:T(8,128)(2,1)S(1)}, bf16[64,2048]{1,0:T(8,128)(2,1)S(1)}, u32[]{:S(2)}, u32[]{:S(2)}) collective-permute-start(bf16[64,2048]{1,0:T(8,128)(2,1)S(1)} %collective-permute-done.11.refs_0_), channel_id=1, source_target_pairs={{0,2},{1,3},{2,0},{3,1},{4,6},{5,7},{6,4},{7,5},{8,10},{9,11},{10,... | collective-permute-start | bytes 786440 | tf_op jit(solution)/shard_map/ppermute | solution.py:384
  228.1 36.3 %collective-permute-start.20 = (bf16[256,2048]{1,0:T(8,128)(2,1)S(1)}, bf16[256,2048]{1,0:T(8,128)(2,1)S(1)}, u32[]{:S(2)}, u32[]{:S(2)}) collective-permute-start(bf16[256,2048]{1,0:T(8,128)(2,1)S(1)} %get-tuple-element.217), channel_id=1, source_target_pairs={{0,2},{1,3},{2,0},{3,1},{4,6},{5,7},{6,4},{7,5},{8,10},{9,11},{10,... | collective-permute-start | bytes 3145736 | tf_op jit(solution)/shard_map/ppermute | solution.py:384
  247.1 39.1 %collective-permute-start.22 = (bf16[256,2048]{1,0:T(8,128)(2,1)S(1)}, bf16[256,2048]{1,0:T(8,128)(2,1)S(1)}, u32[]{:S(2)}, u32[]{:S(2)}) collective-permute-start(bf16[256,2048]{1,0:T(8,128)(2,1)S(1)} %get-tuple-element.237), channel_id=1, source_target_pairs={{0,2},{1,3},{2,0},{3,1},{4,6},{5,7},{6,4},{7,5},{8,10},{9,11},{10,... | collective-permute-start | bytes 3145736 | tf_op jit(solution)/shard_map/ppermute | solution.py:384
  263.2 40.9 %collective-permute-start.23 = (bf16[512,1024]{1,0:T(8,128)(2,1)S(1)}, bf16[512,1024]{1,0:T(8,128)(2,1)S(1)}, u32[]{:S(2)}, u32[]{:S(2)}) collective-permute-start(bf16[512,1024]{1,0:T(8,128)(2,1)S(1)} %get-tuple-element.242), channel_id=1, source_target_pairs={{0,2},{1,3},{2,0},{3,1},{4,6},{5,7},{6,4},{7,5},{8,10},{9,11},{10,... | collective-permute-start | bytes 3145736 | tf_op jit(solution)/shard_map/ppermute | solution.py:384
  264.7 46.9 %collective-permute-start.24 = (bf16[256,2048]{1,0:T(8,128)(2,1)S(1)}, bf16[256,2048]{1,0:T(8,128)(2,1)S(1)}, u32[]{:S(2)}, u32[]{:S(2)}) collective-permute-start(bf16[256,2048]{1,0:T(8,128)(2,1)S(1)} %shard_map.283), channel_id=1, source_target_pairs={{0,16},{1,17},{2,18},{3,19},{4,20},{5,21},{6,22},{7,23},{8,24},{9,... | collective-permute-start | bytes 3145736 | tf_op jit(solution)/shard_map/ppermute | solution.py:384
  311.6 30.2 %collective-permute-start.30 = (bf16[512,1024]{1,0:T(8,128)(2,1)}, bf16[512,1024]{1,0:T(8,128)(2,1)}, u32[]{:S(2)}, u32[]{:S(2)}) collective-permute-start(bf16[512,1024]{1,0:T(8,128)(2,1)} %get-tuple-element.263), channel_id=1, source_target_pairs={{0,2},{1,3},{2,0},{3,1},{4,6},{5,7},{6,4},{7,5},{8,10},{9,11},{10,... | collective-permute-start | bytes 3145736 | tf_op jit(solution)/shard_map/ppermute | solution.py:384
  319.5 55.3 %collective-permute-start.32 = (bf16[512,1024]{1,0:T(8,128)(2,1)}, bf16[512,1024]{1,0:T(8,128)(2,1)}, u32[]{:S(2)}, u32[]{:S(2)}) collective-permute-start(bf16[512,1024]{1,0:T(8,128)(2,1)} %shard_map.287), channel_id=1, source_target_pairs={{0,16},{1,17},{2,18},{3,19},{4,20},{5,21},{6,22},{7,23},{8,24},{9,... | collective-permute-start | bytes 3145736 | tf_op jit(solution)/shard_map/ppermute | solution.py:384
  334.2 40.6 %collective-permute-start.31 = (bf16[512,768]{1,0:T(8,128)(2,1)}, bf16[512,768]{1,0:T(8,128)(2,1)S(1)}, u32[]{:S(2)}, u32[]{:S(2)}) collective-permute-start(bf16[512,768]{1,0:T(8,128)(2,1)} %get-tuple-element.277), channel_id=1, source_target_pairs={{0,2},{1,3},{2,0},{3,1},{4,6},{5,7},{6,4},{7,5},{8,10},{9,11},{10,... | collective-permute-start | bytes 2359304 | tf_op jit(solution)/shard_map/ppermute | solution.py:384
  335.7 39.1 %collective-permute-start.33 = (bf16[256,2048]{1,0:T(8,128)(2,1)}, bf16[256,2048]{1,0:T(8,128)(2,1)S(1)}, u32[]{:S(2)}, u32[]{:S(2)}) collective-permute-start(bf16[256,2048]{1,0:T(8,128)(2,1)} %copy-done.42), channel_id=1, source_target_pairs={{0,4},{1,5},{2,6},{3,7},{4,0},{5,1},{6,2},{7,3},{8,12},{9,13},{10,... | collective-permute-start | bytes 3145736 | tf_op jit(solution)/shard_map/ppermute | solution.py:384
  347.6 42.2 %collective-permute-start.40 = (bf16[256,2048]{1,0:T(8,128)(2,1)}, bf16[256,2048]{1,0:T(8,128)(2,1)}, u32[]{:S(2)}, u32[]{:S(2)}) collective-permute-start(bf16[256,2048]{1,0:T(8,128)(2,1)} %shard_map.291), channel_id=1, source_target_pairs={{0,8},{1,9},{2,10},{3,11},{4,12},{5,13},{6,14},{7,15},{8,0},{9,1},... | collective-permute-start | bytes 3145736 | tf_op jit(solution)/shard_map/ppermute | solution.py:384
  389.8 40.1 %collective-permute-start.34 = (bf16[512,768]{1,0:T(8,128)(2,1)}, bf16[512,768]{1,0:T(8,128)(2,1)}, u32[]{:S(2)}, u32[]{:S(2)}) collective-permute-start(bf16[512,768]{1,0:T(8,128)(2,1)} %copy-done.40), channel_id=1, source_target_pairs={{0,16},{1,17},{2,18},{3,19},{4,20},{5,21},{6,22},{7,23},{8,24},{9,... | collective-permute-start | bytes 2359304 | tf_op jit(solution)/shard_map/ppermute | solution.py:384
  390.0 39.9 %collective-permute-start.35 = (bf16[512,768]{1,0:T(8,128)(2,1)}, bf16[512,768]{1,0:T(8,128)(2,1)}, u32[]{:S(2)}, u32[]{:S(2)}) collective-permute-start(bf16[512,768]{1,0:T(8,128)(2,1)} %copy-done.43), channel_id=1, source_target_pairs={{0,2},{1,3},{2,0},{3,1},{4,6},{5,7},{6,4},{7,5},{8,10},{9,11},{10,... | collective-permute-start | bytes 2359304 | tf_op jit(solution)/shard_map/ppermute | solution.py:384
  391.2 38.7 %collective-permute-start.41 = (bf16[128,2048]{1,0:T(8,128)(2,1)}, bf16[128,2048]{1,0:T(8,128)(2,1)}, u32[]{:S(2)}, u32[]{:S(2)}) collective-permute-start(bf16[128,2048]{1,0:T(8,128)(2,1)} %copy-done.53), channel_id=1, source_target_pairs={{0,2},{1,3},{2,0},{3,1},{4,6},{5,7},{6,4},{7,5},{8,10},{9,11},{10,... | collective-permute-start | bytes 1572872 | tf_op jit(solution)/shard_map/ppermute | solution.py:384
  443.8 33.0 %collective-permute-start.43 = (bf16[256,2048]{1,0:T(8,128)(2,1)}, bf16[256,2048]{1,0:T(8,128)(2,1)}, u32[]{:S(2)}, u32[]{:S(2)}) collective-permute-start(bf16[256,2048]{1,0:T(8,128)(2,1)} %shard_map.295), channel_id=1, source_target_pairs={{0,8},{1,9},{2,10},{3,11},{4,12},{5,13},{6,14},{7,15},{8,0},{9,1},... | collective-permute-start | bytes 3145736 | tf_op jit(solution)/shard_map/ppermute | solution.py:384
  445.8 31.0 %collective-permute-start.44 = (bf16[256,2048]{1,0:T(8,128)(2,1)}, bf16[256,2048]{1,0:T(8,128)(2,1)}, u32[]{:S(2)}, u32[]{:S(2)}) collective-permute-start(bf16[256,2048]{1,0:T(8,128)(2,1)} %get-tuple-element.317), channel_id=1, source_target_pairs={{0,4},{1,5},{2,6},{3,7},{4,0},{5,1},{6,2},{7,3},{8,12},{9,13},{10,... | collective-permute-start | bytes 3145736 | tf_op jit(solution)/shard_map/ppermute | solution.py:384
  447.2 34.2 %collective-permute-start.46 = (bf16[64,2048]{1,0:T(8,128)(2,1)S(1)}, bf16[64,2048]{1,0:T(8,128)(2,1)}, u32[]{:S(2)}, u32[]{:S(2)}) collective-permute-start(bf16[64,2048]{1,0:T(8,128)(2,1)S(1)} %get-tuple-element.341), channel_id=1, source_target_pairs={{0,1},{1,17},{2,3},{3,19},{4,5},{5,21},{6,7},{7,23},{8,9},{9,25},{... | collective-permute-start | bytes 786440 | tf_op jit(solution)/shard_map/ppermute | solution.py:138
  448.5 33.0 %collective-permute-start.45 = (bf16[64,2048]{1,0:T(8,128)(2,1)}, bf16[64,2048]{1,0:T(8,128)(2,1)}, u32[]{:S(2)}, u32[]{:S(2)}) collective-permute-start(bf16[64,2048]{1,0:T(8,128)(2,1)} %get-tuple-element.340), channel_id=1, source_target_pairs={{0,0},{1,16},{2,2},{3,18},{4,4},{5,20},{6,6},{7,22},{8,8},{9,24},{... | collective-permute-start | bytes 786440 | tf_op jit(solution)/shard_map/ppermute | solution.py:138
  (102 other events, 984.7 us)

commit v2 on v1

--- a/solution.py
+++ b/solution.py
@@ -1242,12 +1242,7 @@
     up_got, edge_k = after((up_got, edge_k), qkv_sent)
     up_sum = (up_k0 + up_g0.astype(F32) + up_got.astype(F32)).astype(BF16)
     up_back = lay.to_columns(up_sum.reshape(8, rows, hidden))
-    edge_k, up_sum, out_got = after((edge_k, up_sum, out_got))
-    *edge_g, edge_k = after((*edge_g, edge_k))
-    edge_s1, edge_s0, edge_k = fold_tokens(edge_k, edge_g)
-    edge_g1 = flip(edge_s1, Y)
-
-    edge_k, sums, column_up, column_qkv = after((edge_k, sums, column_up, column_qkv))
+    edge_k, sums, column_up, column_qkv = after((edge_k, sums, column_up, column_qkv), up_sum)
     column_out = jnp.sum(cotangent.astype(F32), axis=0)
     spread_up = lax.dynamic_update_slice(jnp.zeros((HEADS, hidden), F32), column_up, (here, 0))
     spread_up = spread_up.reshape(2, 2, 2, 2, 2, unit).transpose(3, 0, 1, 4, 2, 5)
@@ -1256,6 +1251,11 @@
     sums = restore(sums[:4])
     flat = [v.reshape(n, -1) for v in (sums[0], sums[1], sums[2], sums[3], column_out, spread_qkv, spread_up)]
     flat = jnp.concatenate(flat, axis=1)
+    edge_k, up_sum, out_got, flat = after((edge_k, up_sum, out_got, flat))
+    *edge_g, edge_k = after((*edge_g, edge_k))
+    edge_s1, edge_s0, edge_k = fold_tokens(edge_k, edge_g)
+    edge_g1 = flip(edge_s1, Y)
+
     flat, up_back = after((flat, up_back))
     sums = lax.all_to_all(flat, AXIS, split_axis=0, concat_axis=0, tiled=True)
     qkv_got, qkv_g0, sums, proj_g, edge_k = after((qkv_got, qkv_g0, sums, proj_g, edge_k))

time: 489 us -> 519 us (1.061)
  waiting for transfers between devices: 155 us -> 182 us
    ppermute x43, waiting for transfers between devices: 91.6 us -> 119 us  [flip(): lax.ppermute(value, AXIS, [(d, d ^ 1 << bit) for d in range(lax.axis_size...]
    unnamed x166 -> x170, local copies, waits for them, and re-layouts: 48 us -> 48.9 us
  transfers between devices with their start and end apart: 52 -> 52, of which waited for: 11 -> 10; matrix products, arithmetic and copies ran while one was open for 3% -> 2% of each run, Pallas kernels for 38% -> 36%
where the time goes in v2:
time: 519 us; the launch traced here: 515 us
  Pallas kernels  190 us (37%)
  waiting for transfers between devices  182 us (35%)
  starting transfers between devices  71.2 us (14%)
  local copies, waits for them, and re-layouts  58.5 us (11%)
  other arithmetic  10.4 us (2%)
    ppermute x43, waiting for transfers between devices, flip(): lax.ppermute(value, AXIS, [(d, d ^ 1 << bit) for d in range(lax.axis_size...  119 us
    pallas_call x17, Pallas kernels, call(): pl.pallas_call(body, grid=grid, in_specs=in_specs, out_specs=out_specs, *...  113 us
    pallas_call x8, Pallas kernels, call(): return pl.pallas_call(body, grid_spec=spec, **extra)(scalars, *args)  52.4 us
    unnamed x170, local copies, waits for them, and re-layouts  48.9 us
    all_to_all x1, waiting for transfers between devices, local_tuned(): small = lax.all_to_all(small, AXIS, split_axis=0, concat_axis=0, tiled=True)  41.5 us
    ppermute x43, starting transfers between devices, flip(): lax.ppermute(value, AXIS, [(d, d ^ 1 << bit) for d in range(lax.axis_size...  41.3 us
    all_to_all x1, waiting for transfers between devices, local_tuned(): sums = lax.all_to_all(flat, AXIS, split_axis=0, concat_axis=0, tiled=True)  21.9 us
    pallas_call x1, Pallas kernels, norms(): pl.pallas_call(body, grid=(1,), in_specs=[pl.BlockSpec((8, width), lambda...  13.5 us
  transfers between devices with their start and end apart: 52, of which 10 were waited for; matrix products, arithmetic and copies ran while one was open for 2% of the time, Pallas kernels for 36%

profile of v2, /device:TPU:0, one launch (start us, length us, event | category | flops | bytes accessed | tf_op | source)
XLA Modules:
  0.0 514.6 jit_solution(9857448380864149888)
XLA Ops:
  4.5 5.4 %all-to-all-start = ((bf16[8,64,1792]{2,1,0:T(8,128)(2,1)}), bf16[8,64,1792]{2,1,0:T(8,128)(2,1)}, u32[]{:S(2)}, u32[]{:S(2)}) async-start(bf16[8,64,1792]{2,1,0:T(8,128)(2,1)} %copy-done.9), calls=%async_computation | async-start | bytes 3670016 | tf_op jit(solution)/shard_map/all_to_all | solution.py:186
  19.6 58.3 %collective-permute-done.2.refs_1_ = bf16[256,2048]{1,0:T(8,128)(2,1)} collective-permute-done((bf16[256,2048]{1,0:T(8,128)(2,1)S(1)}, bf16[256,2048]{1,0:T(8,128)(2,1)}, u32[]{:S(2)}, u32[]{:S(2)}) %collective-permute-start.2) | collective-permute-done | bytes 1048608 | tf_op jit(solution)/shard_map/ppermute | solution.py:384
  88.0 3.5 all-to-all-start.1
  93.6 41.5 %all-to-all-done.1.small_ref = bf16[32,16,128]{2,1,0:T(8,128)(2,1)S(1)} async-done(((bf16[32,16,128]{2,1,0:T(8,128)(2,1)}), bf16[32,16,128]{2,1,0:T(8,128)(2,1)S(1)}, u32[]{:S(2)}, u32[]{:S(2)}) %all-to-all-start.1) | async-done | bytes 131104 | tf_op jit(solution)/shard_map/all_to_all | solution.py:1143
  135.1 3.5 shard_map.275.a_ref.xa_ref
  141.8 3.3 collective-permute-start.12
  146.5 6.0 %shard_map.274 = (f32[8,2048]{1,0:T(8,128)S(1)}, f32[1,2048]{1,0:T(1,128)S(1)}, f32[1,1024]{1,0:T(1,128)S(1)}, f32[1,768]{1,0:T(1,128)S(1)}, f32[8,1,256]{2,1,0:...) custom-call(s32[6]{0:T(128)S(1)} %stack.32.place_ref, bf16[32,16,128]{2,1,0:T(8,128)(2,1)S(1)} %all-to-all-done.1.small_ref, ...), custom_call_target="tpu_custom_call" | custom-call | flops 450000000 | bytes 1024 | tf_op jit(solution)/shard_map/pallas_call | solution.py:554
  161.3 3.3 collective-permute-done.10.refs_3_
  170.5 13.5 %shard_map.277 = (bf16[2048,2048]{1,0:T(8,128)(2,1)}, bf16[2048,2048]{1,0:T(8,128)(2,1)}, f32[2048,128]{1,0:T(8,128)S(1)}) custom-call(f32[8,2048]{1,0:T(8,128)S(1)} %get-tuple-element.197.v_ref, bf16[1024,2048]{1,0:T(8,128)(2,1)} %shard_map.275.a_ref.xa_ref, bf16[1024,2048]{1,0:T(8,128)(2,1)} %collective-permute-done.14.b_ref.xb_ref), custom_call_target="tpu_custom_call" | custom-call | flops 5400000000 | bytes 1024 | tf_op jit(solution)/shard_map/pallas_call | solution.py:679
  185.1 16.2 %shard_map.278 = (bf16[2048,1024]{1,0:T(8,128)(2,1)S(1)}, f32[2048,1024]{1,0:T(8,128)}) custom-call(bf16[2048,2048]{1,0:T(8,128)(2,1)} %get-tuple-element.199.s_ref.l_ref, bf16[512,1024]{1,0:T(8,128)(2,1)} %bitcast.7.refs_0_, bf16[512,1024]{1,0:T(8,128)(2,1)} %bitcast.8.refs_1_, bf16[512,1024]{1,0:T(8,128)(2,1)} %bitcast.9.refs_2_, ...), custom_call_target="tpu_custom_call" | custom-call | flops 7200000000 | bytes 1024 | tf_op jit(solution)/shard_map/pallas_call | solution.py:395
  201.3 3.6 collective-permute-done.15
  208.9 14.7 %shard_map.280 = (bf16[256,2048]{1,0:T(8,128)(2,1)S(1)}, bf16[256,2048]{1,0:T(8,128)(2,1)S(1)}, f32[256,2048]{1,0:T(8,128)S(1)}, f32[256,2048]{1,0:T(8,128)S(1)}) custom-call(s32[2]{0:T(128)S(1)} %pad_add_fusion.mine_ref, bf16[2048,1024]{1,0:T(8,128)(2,1)S(1)} %get-tuple-element.241.l_ref.a_ref, bf16[1024,2048]{1,0:T(8,128)(2,1)} %copy-done, ...), custom_call_target="tpu_custom_call" | custom-call | flops 6750000128 | bytes 1024 | tf_op jit(solution)/shard_map/pallas_call | solution.py:397
  231.3 12.5 %shard_map.281 = (bf16[2048,1024]{1,0:T(8,128)(2,1)S(1)}, f32[1,1024]{1,0:T(1,128)S(1)}) custom-call(bf16[1024,2048]{1,0:T(8,128)(2,1)S(1)} %copy-done.1, bf16[1024,2048]{1,0:T(8,128)(2,1)S(1)} %copy-done.11, bf16[1024,2048]{1,0:T(8,128)(2,1)} %copy-done.13, f32[2048,1024]{1,0:T(8,128)} %get-tuple-element.220.slope_ref), custom_call_target="tpu_custom_call" | custom-call | flops 6300000256 | bytes 1024 | tf_op jit(solution)/shard_map/pallas_call | solution.py:395
  250.1 13.0 %shard_map.282 = (bf16[512,1024]{1,0:T(8,128)(2,1)S(1)}, bf16[512,1024]{1,0:T(8,128)(2,1)}, f32[512,1024]{1,0:T(8,128)S(1)}, f32[512,1024]{1,0:T(8,128)S(1)}) custom-call(s32[2]{0:T(128)S(1)} %pad_add_fusion.mine_ref, bf16[2048,2048]{1,0:T(8,128)(2,1)} %get-tuple-element.199.s_ref.l_ref, bf16[2048,1024]{1,0:T(8,128)(2,1)S(1)} %copy-done.59), custom_call_target="tpu_custom_call" | custom-call | flops 5400000000 | bytes 1024 | tf_op jit(solution)/shard_map/pallas_call | solution.py:397
  266.8 17.8 %shard_map.285 = (bf16[2048,256]{1,0:T(8,128)(2,1)S(1)}, bf16[2048,768]{1,0:T(8,128)(2,1)S(1)}, f32[1,768]{1,0:T(1,128)S(1)}) custom-call(bf16[2048,2048]{1,0:T(8,128)(2,1)} %get-tuple-element.227.f_ref.l_ref, bf16[512,768]{1,0:T(8,128)(2,1)S(1)} %bitcast.32, bf16[512,768]{1,0:T(8,128)(2,1)S(1)} %bitcast.34, bf16[512,768]{1,0:T(8,128)(2,1)S(1)} %bitcast.36, ...), custom_call_target="tpu_custom_call" | custom-call | flops 7649999872 | bytes 1024 | tf_op jit(solution)/shard_map/pallas_call | solution.py:395
  286.3 15.2 %shard_map.286 = (bf16[256,2048]{1,0:T(8,128)(2,1)S(1)}, bf16[256,2048]{1,0:T(8,128)(2,1)S(1)}, bf16[256,2048]{1,0:T(8,128)(2,1)S(1)}, bf16[256,2048]{1,0:T(8,128)(2,1)S(1)}, bf16[1024,2048]{1,0:T(8,128)(2,1)S(1)}) custom-call(bf16[2048,1024]{1,0:T(8,128)(2,1)} %copy-done.68, bf16[1024,2048]{1,0:T(8,128)(2,1)} %copy-done.13, ...), custom_call_target="tpu_custom_call" | custom-call | flops 7200000000 | bytes 1024 | tf_op jit(solution)/shard_map/pallas_call | solution.py:395
  304.5 7.1 %collective-permute-done.24.refs_2_ = bf16[256,2048]{1,0:T(8,128)(2,1)S(1)} collective-permute-done((bf16[256,2048]{1,0:T(8,128)(2,1)S(1)}, bf16[256,2048]{1,0:T(8,128)(2,1)S(1)}, u32[]{:S(2)}, u32[]{:S(2)}) %collective-permute-start.24) | collective-permute-done | bytes 1048608 | tf_op jit(solution)/shard_map/ppermute | solution.py:384
  313.3 4.3 shard_map.288
  321.9 11.1 %shard_map.289 = (bf16[512,768]{1,0:T(8,128)(2,1)}, bf16[512,768]{1,0:T(8,128)(2,1)S(1)}, f32[512,768]{1,0:T(8,128)S(1)}, f32[512,768]{1,0:T(8,128)S(1)}) custom-call(s32[2]{0:T(128)S(1)} %pad_add_fusion.mine_ref, bf16[2048,2048]{1,0:T(8,128)(2,1)} %get-tuple-element.227.f_ref.l_ref, bf16[2048,768]{1,0:T(8,128)(2,1)S(1)} %copy-done.65), custom_call_target="tpu_custom_call" | custom-call | flops 4499999744 | bytes 1024 | tf_op jit(solution)/shard_map/pallas_call | solution.py:397
  337.9 3.8 shard_map.290
  341.7 3.2 collective-permute-done.29.g_ref
  347.6 26.3 %shard_map.292 = (bf16[256,2048]{1,0:T(8,128)(2,1)S(1)}, bf16[256,2048]{1,0:T(8,128)(2,1)S(1)}, bf16[256,2048]{1,0:T(8,128)(2,1)}, bf16[256,2048]{1,0:T(8,128)(2...) custom-call(bf16[2048,1024]{1,0:T(8,128)(2,1)} %copy-done.58, bf16[2048,768]{1,0:T(8,128)(2,1)} %copy-done.64, ...), custom_call_target="tpu_custom_call" | custom-call | flops 12600000512 | bytes 1024 | tf_op jit(solution)/shard_map/pallas_call | solution.py:395
  375.2 3.8 add_convert_fusion
  379.0 3.6 all-to-all-start.2
  385.8 33.7 %collective-permute-done.36.refs_4_ = bf16[256,2048]{1,0:T(8,128)(2,1)} collective-permute-done((bf16[256,2048]{1,0:T(8,128)(2,1)}, bf16[256,2048]{1,0:T(8,128)(2,1)}, u32[]{:S(2)}, u32[]{:S(2)}) %collective-permute-start.36) | collective-permute-done | bytes 1048608 | tf_op jit(solution)/shard_map/ppermute | solution.py:384
  423.8 4.7 all-to-all-start.3
  428.6 6.0 %shard_map.294 = (bf16[256,2048]{1,0:T(8,128)(2,1)}, bf16[256,2048]{1,0:T(8,128)(2,1)}, f32[512,2048]{1,0:T(8,128)S(1)}) custom-call(bf16[1024,2048]{1,0:T(8,128)(2,1)} %get-tuple-element.304.k_ref, bf16[256,2048]{1,0:T(8,128)(2,1)} %collective-permute-done.38.refs_0_, bf16[256,2048]{1,0:T(8,128)(2,1)} %collective-permute-done.39.refs_1_, ...), custom_call_target="tpu_custom_call" | custom-call | flops 2249999872 | bytes 1024 | tf_op jit(solution)/shard_map/pallas_call | solution.py:395
  438.4 21.9 %all-to-all-done.3 = f32[32,1,768]{2,1,0:T(1,128)S(1)} async-done(((f32[32,1,768]{2,1,0:T(1,128)}), f32[32,1,768]{2,1,0:T(1,128)S(1)}, u32[]{:S(2)}, u32[]{:S(2)}) %all-to-all-start.3) | async-done | bytes 98336 | tf_op jit(solution)/shard_map/all_to_all | solution.py:1260
  463.3 4.2 all-to-all-start.4
  478.9 3.6 collective-permute-start.45
  498.1 9.1 %collective-permute-done.43.b_ref = bf16[256,2048]{1,0:T(8,128)(2,1)} collective-permute-done((bf16[256,2048]{1,0:T(8,128)(2,1)}, bf16[256,2048]{1,0:T(8,128)(2,1)}, u32[]{:S(2)}, u32[]{:S(2)}) %collective-permute-start.43) | collective-permute-done | bytes 1048608 | tf_op jit(solution)/shard_map/ppermute | solution.py:384
  507.3 4.6 shard_map.300
  (313 shorter events, 130.5 us)
Async XLA Ops:
  4.5 73.4 %all-to-all-start = ((bf16[8,64,1792]{2,1,0:T(8,128)(2,1)}), bf16[8,64,1792]{2,1,0:T(8,128)(2,1)}, u32[]{:S(2)}, u32[]{:S(2)}) async-start(bf16[8,64,1792]{2,1,0:T(8,128)(2,1)} %copy-done.9), calls=%async_computation | async-start | bytes 3670016 | tf_op jit(solution)/shard_map/all_to_all | solution.py:186
  10.8 67.1 %collective-permute-start.2 = (bf16[256,2048]{1,0:T(8,128)(2,1)S(1)}, bf16[256,2048]{1,0:T(8,128)(2,1)}, u32[]{:S(2)}, u32[]{:S(2)}) collective-permute-start(bf16[256,2048]{1,0:T(8,128)(2,1)S(1)} %shard_map.273.refs_0_.x_ref), channel_id=1, source_target_pairs={{0,8},{1,9},{2,10},{3,11},{4,12},{5,13},{6,14},{7,15},{8,0},{9,1},... | collective-permute-start | bytes 3145736 | tf_op jit(solution)/shard_map/ppermute | solution.py:384
  12.9 65.0 %collective-permute-start.3 = (bf16[256,2048]{1,0:T(8,128)(2,1)S(1)}, bf16[256,2048]{1,0:T(8,128)(2,1)}, u32[]{:S(2)}, u32[]{:S(2)}) collective-permute-start(bf16[256,2048]{1,0:T(8,128)(2,1)S(1)} %shard_map.273.refs_0_.x_ref), channel_id=1, source_target_pairs={{0,4},{1,5},{2,6},{3,7},{4,0},{5,1},{6,2},{7,3},{8,12},{9,13},{10,... | collective-permute-start | bytes 3145736 | tf_op jit(solution)/shard_map/ppermute | solution.py:384
  14.4 63.5 %collective-permute-start = (bf16[256,2048]{1,0:T(8,128)(2,1)}, bf16[256,2048]{1,0:T(8,128)(2,1)S(1)}, u32[]{:S(2)}, u32[]{:S(2)}) collective-permute-start(bf16[256,2048]{1,0:T(8,128)(2,1)} %refs_0_.2), channel_id=1, source_target_pairs={{0,16},{1,17},{2,18},{3,19},{4,20},{5,21},{6,22},{7,23},{8,24},{9,... | collective-permute-start | bytes 3145736 | tf_op jit(solution)/shard_map/ppermute | solution.py:384
  17.4 60.5 %collective-permute-start.1 = (bf16[256,2048]{1,0:T(8,128)(2,1)}, bf16[256,2048]{1,0:T(8,128)(2,1)}, u32[]{:S(2)}, u32[]{:S(2)}) collective-permute-start(bf16[256,2048]{1,0:T(8,128)(2,1)} %refs_0_.2), channel_id=1, source_target_pairs={{0,2},{1,3},{2,0},{3,1},{4,6},{5,7},{6,4},{7,5},{8,10},{9,11},{10,... | collective-permute-start | bytes 3145736 | tf_op jit(solution)/shard_map/ppermute | solution.py:384
  18.8 59.0 %collective-permute-start.4 = (bf16[256,2048]{1,0:T(8,128)(2,1)S(1)}, bf16[256,2048]{1,0:T(8,128)(2,1)}, u32[]{:S(2)}, u32[]{:S(2)}) collective-permute-start(bf16[256,2048]{1,0:T(8,128)(2,1)S(1)} %copy-done.8), channel_id=1, source_target_pairs={{0,4},{1,5},{2,6},{3,7},{4,0},{5,1},{6,2},{7,3},{8,12},{9,13},{10,... | collective-permute-start | bytes 3145736 | tf_op jit(solution)/shard_map/ppermute | solution.py:384
  80.9 54.1 %collective-permute-start.5 = (bf16[8,64,1024]{2,1,0:T(8,128)(2,1)}, bf16[8,64,1024]{2,1,0:T(8,128)(2,1)}, u32[]{:S(2)}, u32[]{:S(2)}) collective-permute-start(bf16[8,64,1024]{2,1,0:T(8,128)(2,1)} %slice.46), channel_id=1, source_target_pairs={{0,16},{1,17},{2,18},{3,19},{4,20},{5,21},{6,22},{7,23},{8,24},{9,... | collective-permute-start | bytes 3145736 | tf_op jit(solution)/shard_map/ppermute | solution.py:384
  83.7 51.3 %collective-permute-start.6 = (bf16[8,64,1024]{2,1,0:T(8,128)(2,1)}, bf16[8,64,1024]{2,1,0:T(8,128)(2,1)}, u32[]{:S(2)}, u32[]{:S(2)}) collective-permute-start(bf16[8,64,1024]{2,1,0:T(8,128)(2,1)} %slice.46), channel_id=1, source_target_pairs={{0,2},{1,3},{2,0},{3,1},{4,6},{5,7},{6,4},{7,5},{8,10},{9,11},{10,... | collective-permute-start | bytes 3145736 | tf_op jit(solution)/shard_map/ppermute | solution.py:384
  85.2 49.8 %collective-permute-start.7 = (bf16[256,2048]{1,0:T(8,128)(2,1)}, bf16[256,2048]{1,0:T(8,128)(2,1)}, u32[]{:S(2)}, u32[]{:S(2)}) collective-permute-start(bf16[256,2048]{1,0:T(8,128)(2,1)} %collective-permute-done.2.refs_1_), channel_id=1, source_target_pairs={{0,4},{1,5},{2,6},{3,7},{4,0},{5,1},{6,2},{7,3},{8,12},{9,13},{10,... | collective-permute-start | bytes 3145736 | tf_op jit(solution)/shard_map/ppermute | solution.py:384
  85.8 49.3 %collective-permute-start.8 = (bf16[256,2048]{1,0:T(8,128)(2,1)S(1)}, bf16[256,2048]{1,0:T(8,128)(2,1)}, u32[]{:S(2)}, u32[]{:S(2)}) collective-permute-start(bf16[256,2048]{1,0:T(8,128)(2,1)S(1)} %copy-done.8), channel_id=1, source_target_pairs={{0,8},{1,9},{2,10},{3,11},{4,12},{5,13},{6,14},{7,15},{8,0},{9,1},... | collective-permute-start | bytes 3145736 | tf_op jit(solution)/shard_map/ppermute | solution.py:384
  87.4 47.6 %collective-permute-start.9 = (bf16[256,2048]{1,0:T(8,128)(2,1)S(1)}, bf16[256,2048]{1,0:T(8,128)(2,1)}, u32[]{:S(2)}, u32[]{:S(2)}) collective-permute-start(bf16[256,2048]{1,0:T(8,128)(2,1)S(1)} %collective-permute-done.refs_2_), channel_id=1, source_target_pairs={{0,2},{1,3},{2,0},{3,1},{4,6},{5,7},{6,4},{7,5},{8,10},{9,11},{10,... | collective-permute-start | bytes 3145736 | tf_op jit(solution)/shard_map/ppermute | solution.py:384
  88.0 47.1 %all-to-all-start.1 = ((bf16[32,16,128]{2,1,0:T(8,128)(2,1)}), bf16[32,16,128]{2,1,0:T(8,128)(2,1)S(1)}, u32[]{:S(2)}, u32[]{:S(2)}) async-start(bf16[32,16,128]{2,1,0:T(8,128)(2,1)} %broadcast_in_dim.14), calls=%async_computation.1 | async-start | bytes 262144 | tf_op jit(solution)/shard_map/all_to_all | solution.py:1143
  167.1 38.7 %collective-permute-start.18 = (bf16[1024,2048]{1,0:T(8,128)(2,1)S(1)}, bf16[1024,2048]{1,0:T(8,128)(2,1)S(1)}, u32[]{:S(2)}, u32[]{:S(2)}) collective-permute-start(bf16[1024,2048]{1,0:T(8,128)(2,1)S(1)} %shard_map.279.refs_0_.ga_ref), channel_id=1, source_target_pairs={{0,1},{1,0},{2,3},{3,2},{4,5},{5,4},{6,7},{7,6},{8,9},{9,8},{10,11... | collective-permute-start | bytes 12582920 | tf_op jit(solution)/shard_map/ppermute | solution.py:384
  167.2 37.7 %collective-permute-start.15 = (bf16[8,64,768]{2,1,0:T(8,128)(2,1)S(1)}, bf16[8,64,768]{2,1,0:T(8,128)(2,1)S(1)}, u32[]{:S(2)}, u32[]{:S(2)}) collective-permute-start(bf16[8,64,768]{2,1,0:T(8,128)(2,1)S(1)} %copy-done.39), channel_id=1, source_target_pairs={{0,16},{1,17},{2,18},{3,19},{4,20},{5,21},{6,22},{7,23},{8,24},{9,... | collective-permute-start | bytes 2359304 | tf_op jit(solution)/shard_map/ppermute | solution.py:384
  168.5 36.4 %collective-permute-start.16 = (bf16[8,64,768]{2,1,0:T(8,128)(2,1)S(1)}, bf16[8,64,768]{2,1,0:T(8,128)(2,1)S(1)}, u32[]{:S(2)}, u32[]{:S(2)}) collective-permute-start(bf16[8,64,768]{2,1,0:T(8,128)(2,1)S(1)} %copy-done.39), channel_id=1, source_target_pairs={{0,2},{1,3},{2,0},{3,1},{4,6},{5,7},{6,4},{7,5},{8,10},{9,11},{10,... | collective-permute-start | bytes 2359304 | tf_op jit(solution)/shard_map/ppermute | solution.py:384
  228.1 36.3 %collective-permute-start.20 = (bf16[256,2048]{1,0:T(8,128)(2,1)S(1)}, bf16[256,2048]{1,0:T(8,128)(2,1)S(1)}, u32[]{:S(2)}, u32[]{:S(2)}) collective-permute-start(bf16[256,2048]{1,0:T(8,128)(2,1)S(1)} %get-tuple-element.218), channel_id=1, source_target_pairs={{0,2},{1,3},{2,0},{3,1},{4,6},{5,7},{6,4},{7,5},{8,10},{9,11},{10,... | collective-permute-start | bytes 3145736 | tf_op jit(solution)/shard_map/ppermute | solution.py:384
  247.2 39.1 %collective-permute-start.22 = (bf16[256,2048]{1,0:T(8,128)(2,1)S(1)}, bf16[256,2048]{1,0:T(8,128)(2,1)S(1)}, u32[]{:S(2)}, u32[]{:S(2)}) collective-permute-start(bf16[256,2048]{1,0:T(8,128)(2,1)S(1)} %get-tuple-element.238), channel_id=1, source_target_pairs={{0,2},{1,3},{2,0},{3,1},{4,6},{5,7},{6,4},{7,5},{8,10},{9,11},{10,... | collective-permute-start | bytes 3145736 | tf_op jit(solution)/shard_map/ppermute | solution.py:384
  263.1 40.9 %collective-permute-start.23 = (bf16[512,1024]{1,0:T(8,128)(2,1)S(1)}, bf16[512,1024]{1,0:T(8,128)(2,1)S(1)}, u32[]{:S(2)}, u32[]{:S(2)}) collective-permute-start(bf16[512,1024]{1,0:T(8,128)(2,1)S(1)} %get-tuple-element.243), channel_id=1, source_target_pairs={{0,2},{1,3},{2,0},{3,1},{4,6},{5,7},{6,4},{7,5},{8,10},{9,11},{10,... | collective-permute-start | bytes 3145736 | tf_op jit(solution)/shard_map/ppermute | solution.py:384
  264.7 46.9 %collective-permute-start.24 = (bf16[256,2048]{1,0:T(8,128)(2,1)S(1)}, bf16[256,2048]{1,0:T(8,128)(2,1)S(1)}, u32[]{:S(2)}, u32[]{:S(2)}) collective-permute-start(bf16[256,2048]{1,0:T(8,128)(2,1)S(1)} %shard_map.283), channel_id=1, source_target_pairs={{0,16},{1,17},{2,18},{3,19},{4,20},{5,21},{6,22},{7,23},{8,24},{9,... | collective-permute-start | bytes 3145736 | tf_op jit(solution)/shard_map/ppermute | solution.py:384
  319.5 55.5 %collective-permute-start.32 = (bf16[512,1024]{1,0:T(8,128)(2,1)}, bf16[512,1024]{1,0:T(8,128)(2,1)}, u32[]{:S(2)}, u32[]{:S(2)}) collective-permute-start(bf16[512,1024]{1,0:T(8,128)(2,1)} %shard_map.287), channel_id=1, source_target_pairs={{0,16},{1,17},{2,18},{3,19},{4,20},{5,21},{6,22},{7,23},{8,24},{9,... | collective-permute-start | bytes 3145736 | tf_op jit(solution)/shard_map/ppermute | solution.py:384
  334.1 40.8 %collective-permute-start.31 = (bf16[512,768]{1,0:T(8,128)(2,1)}, bf16[512,768]{1,0:T(8,128)(2,1)S(1)}, u32[]{:S(2)}, u32[]{:S(2)}) collective-permute-start(bf16[512,768]{1,0:T(8,128)(2,1)} %get-tuple-element.278), channel_id=1, source_target_pairs={{0,2},{1,3},{2,0},{3,1},{4,6},{5,7},{6,4},{7,5},{8,10},{9,11},{10,... | collective-permute-start | bytes 2359304 | tf_op jit(solution)/shard_map/ppermute | solution.py:384
  335.7 39.2 %collective-permute-start.33 = (bf16[256,2048]{1,0:T(8,128)(2,1)}, bf16[256,2048]{1,0:T(8,128)(2,1)S(1)}, u32[]{:S(2)}, u32[]{:S(2)}) collective-permute-start(bf16[256,2048]{1,0:T(8,128)(2,1)} %copy-done.44), channel_id=1, source_target_pairs={{0,4},{1,5},{2,6},{3,7},{4,0},{5,1},{6,2},{7,3},{8,12},{9,13},{10,... | collective-permute-start | bytes 3145736 | tf_op jit(solution)/shard_map/ppermute | solution.py:384
  379.0 44.1 %all-to-all-start.2 = ((bf16[8,64,1024]{2,1,0:T(8,128)(2,1)}), bf16[8,64,1024]{2,1,0:T(8,128)(2,1)S(1)}, u32[]{:S(2)}, u32[]{:S(2)}) async-start(bf16[8,64,1024]{2,1,0:T(8,128)(2,1)} %bitcast.40), calls=%async_computation.2 | async-start | bytes 2097152 | tf_op jit(solution)/shard_map/all_to_all | solution.py:186
  382.6 37.0 %collective-permute-start.36 = (bf16[256,2048]{1,0:T(8,128)(2,1)}, bf16[256,2048]{1,0:T(8,128)(2,1)}, u32[]{:S(2)}, u32[]{:S(2)}) collective-permute-start(bf16[256,2048]{1,0:T(8,128)(2,1)} %copy-done.35), channel_id=1, source_target_pairs={{0,8},{1,9},{2,10},{3,11},{4,12},{5,13},{6,14},{7,15},{8,0},{9,1},... | collective-permute-start | bytes 3145736 | tf_op jit(solution)/shard_map/ppermute | solution.py:384
  384.5 35.5 %collective-permute-start.38 = (bf16[256,2048]{1,0:T(8,128)(2,1)}, bf16[256,2048]{1,0:T(8,128)(2,1)}, u32[]{:S(2)}, u32[]{:S(2)}) collective-permute-start(bf16[256,2048]{1,0:T(8,128)(2,1)} %copy-done.43), channel_id=1, source_target_pairs={{0,1},{1,0},{2,3},{3,2},{4,5},{5,4},{6,7},{7,6},{8,9},{9,8},{10,11... | collective-permute-start | bytes 3145736 | tf_op jit(solution)/shard_map/ppermute | solution.py:384
  384.5 37.3 %collective-permute-start.39 = (bf16[256,2048]{1,0:T(8,128)(2,1)}, bf16[256,2048]{1,0:T(8,128)(2,1)}, u32[]{:S(2)}, u32[]{:S(2)}) collective-permute-start(bf16[256,2048]{1,0:T(8,128)(2,1)} %copy-done.42), channel_id=1, source_target_pairs={{0,1},{1,0},{2,3},{3,2},{4,5},{5,4},{6,7},{7,6},{8,9},{9,8},{10,11... | collective-permute-start | bytes 3145736 | tf_op jit(solution)/shard_map/ppermute | solution.py:384
  385.0 38.1 %collective-permute-start.40 = (bf16[256,2048]{1,0:T(8,128)(2,1)}, bf16[256,2048]{1,0:T(8,128)(2,1)}, u32[]{:S(2)}, u32[]{:S(2)}) collective-permute-start(bf16[256,2048]{1,0:T(8,128)(2,1)} %get-tuple-element.301), channel_id=1, source_target_pairs={{0,1},{1,0},{2,3},{3,2},{4,5},{5,4},{6,7},{7,6},{8,9},{9,8},{10,11... | collective-permute-start | bytes 3145736 | tf_op jit(solution)/shard_map/ppermute | solution.py:384
  385.0 38.1 %collective-permute-start.41 = (bf16[256,2048]{1,0:T(8,128)(2,1)}, bf16[256,2048]{1,0:T(8,128)(2,1)}, u32[]{:S(2)}, u32[]{:S(2)}) collective-permute-start(bf16[256,2048]{1,0:T(8,128)(2,1)} %get-tuple-element.302), channel_id=1, source_target_pairs={{0,1},{1,0},{2,3},{3,2},{4,5},{5,4},{6,7},{7,6},{8,9},{9,8},{10,11... | collective-permute-start | bytes 3145736 | tf_op jit(solution)/shard_map/ppermute | solution.py:384
  419.5 40.8 %collective-permute-start.34 = (bf16[512,768]{1,0:T(8,128)(2,1)}, bf16[512,768]{1,0:T(8,128)(2,1)}, u32[]{:S(2)}, u32[]{:S(2)}) collective-permute-start(bf16[512,768]{1,0:T(8,128)(2,1)} %copy-done.41), channel_id=1, source_target_pairs={{0,16},{1,17},{2,18},{3,19},{4,20},{5,21},{6,22},{7,23},{8,24},{9,... | collective-permute-start | bytes 2359304 | tf_op jit(solution)/shard_map/ppermute | solution.py:384
  420.0 40.3 %collective-permute-start.35 = (bf16[512,768]{1,0:T(8,128)(2,1)}, bf16[512,768]{1,0:T(8,128)(2,1)}, u32[]{:S(2)}, u32[]{:S(2)}) collective-permute-start(bf16[512,768]{1,0:T(8,128)(2,1)} %copy-done.45), channel_id=1, source_target_pairs={{0,2},{1,3},{2,0},{3,1},{4,6},{5,7},{6,4},{7,5},{8,10},{9,11},{10,... | collective-permute-start | bytes 2359304 | tf_op jit(solution)/shard_map/ppermute | solution.py:384
  421.8 38.5 %collective-permute-start.37 = (bf16[128,2048]{1,0:T(8,128)(2,1)}, bf16[128,2048]{1,0:T(8,128)(2,1)}, u32[]{:S(2)}, u32[]{:S(2)}) collective-permute-start(bf16[128,2048]{1,0:T(8,128)(2,1)} %copy-done.55), channel_id=1, source_target_pairs={{0,2},{1,3},{2,0},{3,1},{4,6},{5,7},{6,4},{7,5},{8,10},{9,11},{10,... | collective-permute-start | bytes 1572872 | tf_op jit(solution)/shard_map/ppermute | solution.py:384
  423.8 36.5 %all-to-all-start.3 = ((f32[32,1,768]{2,1,0:T(1,128)}), f32[32,1,768]{2,1,0:T(1,128)S(1)}, u32[]{:S(2)}, u32[]{:S(2)}) async-start(f32[32,1,768]{2,1,0:T(1,128)} %copy.39), calls=%async_computation.3 | async-start | bytes 196608 | tf_op jit(solution)/shard_map/all_to_all | solution.py:1260
  (104 other events, 1071.0 us)
